TPU v7x, 128 devices: a whole 4x4x4 slice. The times are simulated.
128 devices in a mesh: blk: 32 (over z, y, core), pair: 4 (over x).
Axes of the slice: x: 4, y: 4, z: 4, core: 2. Of those that a mesh axis runs over, the one named last changes fastest.
Arguments:
- basis: float32 [8, 256, 510, 128], P(None, ('blk', 'pair'))
- mie_coeffs: float32 [256, 510, 128], P(('blk', 'pair')), may hold values from -8 to 8
- rot_table: bfloat16 [8, 510, 510], replicated, may hold values from -0.25 to 0.25
- axial_table: bfloat16 [8, 2, 510, 510], replicated, may hold values from -0.1875 to 0.1875
- pair_table: int32 [32, 128, 3], P('blk'), may hold values from 0 to 23, as said below
- pair_count: int32 [32], P('blk'), may hold values from 32 to 128, as said below
Outputs:
- projections: float32 [2, 8], replicated
- next_basis: float32 [256, 510, 128], P(('blk', 'pair'))
Inputs may be any that keep to these rules, and one draw needn't show every extreme that they name: `pair_table`: row p of blk index i is (a, b, g): a names one of the 8 blocks of blk index i; b counts from the first block of blk index i - 1 and is never a + 8; on blk index 0, b >= 8; on the last, b < 16; g < 8. Rows from pair_count on are ignored. `pair_count`: some blk index lists all 128 rows.
All inputs are finite; a program needn't handle non-finite values.
Results may differ from a plain program's by a relative error of at most 0.0003.
Values may be sent and summed in bfloat16 or wider, within the bound.
A program may use at most 128 MiB of HBM per device.

v0:
```python
import jax
import jax.numpy as jnp
from jax import lax
from jax.sharding import PartitionSpec as P

batch_pairs = 8


def extended(value, sides, width):
    for axis, dim in sides:
        count, length = (lax.axis_size(axis), value.shape[dim])
        up = [(i, (i + 1) % count) for i in range(count - 1)]
        down = [(j, i) for i, j in up]
        last = lax.slice_in_dim(value, length - width, length, axis=dim)
        leading = lax.slice_in_dim(value, 0, width, axis=dim)
        before = lax.ppermute(last, axis, up)
        after = lax.ppermute(leading, axis, down)
        value = jnp.concatenate([before, value, after], axis=dim)
    return value


def shifted(value, axis, steps):
    count = lax.axis_size(axis)
    leading, last = (max(0, -steps), min(count, count - steps))
    return lax.ppermute(value, axis, [(source, source + steps) for source in range(leading, last)])


def swap_parts(packed):
    half_width = packed.shape[-1] // 2
    return jnp.concatenate([-packed[..., half_width:], packed[..., :half_width]], axis=-1)


def complex_product(left, right):
    half_width = left.shape[-1] // 2
    left_real, left_imag = (left[..., :half_width], left[..., half_width:])
    right_real, right_imag = (right[..., :half_width], right[..., half_width:])
    return jnp.concatenate(
        [
            left_real * right_real - left_imag * right_imag,
            left_real * right_imag + left_imag * right_real,
        ],
        axis=-1,
    )


def translate(rotation, axial_pair, source, transposed):
    turned = jnp.einsum(
        "pij,pjk->pik", rotation, source, preferred_element_type=jnp.float32
    ).astype(jnp.bfloat16)
    stacked = jnp.stack([turned, swap_parts(turned)], axis=1)
    if transposed:
        moved = jnp.einsum(
            "pcji,pcjk->pik", axial_pair, stacked, preferred_element_type=jnp.float32
        )
    else:
        moved = jnp.einsum(
            "pcij,pcjk->pik", axial_pair, stacked, preferred_element_type=jnp.float32
        )
    moved = moved.astype(jnp.bfloat16)
    return jnp.einsum("pji,pjk->pik", rotation, moved, preferred_element_type=jnp.float32)


def shards(basis, mie_coeffs, rot_table, axial_table, pair_table, pair_count):
    vector_count = basis.shape[0]
    quarter = basis.shape[1]
    mode_count = basis.shape[2]
    column_count = basis.shape[3]
    pair_ways = lax.axis_size("pair")
    blk_ways = lax.axis_size("blk")
    own_count = quarter * pair_ways
    current = basis[vector_count - 1].astype(jnp.bfloat16)
    own_coeff = lax.all_gather(current, "pair", axis=0, tiled=True)
    window = extended(own_coeff, (("blk", 0),), own_count)
    pair_rows = pair_table[0]
    live_total = pair_count[0]
    slot_total = pair_rows.shape[0]
    share = slot_total // pair_ways
    member = lax.axis_index("pair")
    live_here = jnp.clip(live_total - member * share, 0, share)
    first_slot = member * share
    stride_length = 1
    group_total = (live_here + batch_pairs - 1) // batch_pairs

    def accumulate(group_index, scattered):
        ordinal = group_index * batch_pairs + jnp.arange(batch_pairs, dtype=jnp.int32)
        active = ordinal < live_here
        chosen = pair_rows[jnp.minimum(first_slot + stride_length * ordinal, slot_total - 1)]
        target_rows = chosen[:, 0] + own_count
        source_rows = chosen[:, 1]
        table_rows = chosen[:, 2]
        rotation = rot_table[table_rows]
        axial_pair = axial_table[table_rows]
        forward = translate(rotation, axial_pair, window[source_rows], False)
        backward = translate(rotation, axial_pair, window[target_rows], True)
        forward = jnp.where(active[:, None, None], forward, jnp.float32(0.0))
        backward = jnp.where(active[:, None, None], backward, jnp.float32(0.0))
        return scattered.at[target_rows].add(forward).at[source_rows].add(backward)

    start_field = jnp.zeros((3 * own_count, mode_count, own_coeff.shape[2]), jnp.float32)
    scattered = lax.fori_loop(0, group_total, accumulate, start_field)
    lower_part = shifted(scattered[:own_count].astype(jnp.bfloat16), "blk", -1).astype(jnp.float32)
    upper_part = shifted(scattered[2 * own_count :].astype(jnp.bfloat16), "blk", 1).astype(
        jnp.float32
    )
    middle = scattered[own_count : 2 * own_count] + lower_part + upper_part
    field_here = lax.psum_scatter(
        middle.astype(jnp.bfloat16), "pair", scatter_dimension=0, tiled=True
    ).astype(jnp.float32)
    image = basis[vector_count - 1] - complex_product(mie_coeffs, field_here)
    mean_scale = 1.0 / (own_count * blk_ways * mode_count * column_count)
    highest = lax.Precision.HIGHEST
    real_local = jnp.einsum("kbcs,bcs->k", basis, image, precision=highest)
    imag_local = -jnp.einsum("kbcs,bcs->k", basis, swap_parts(image), precision=highest)
    dots = lax.psum(jnp.stack([real_local, imag_local]), ("blk", "pair")) * mean_scale
    real_part, imag_part = (dots[0], dots[1])
    remainder = image - jnp.einsum("k,kbcs->bcs", real_part, basis, precision=highest)
    remainder = remainder - jnp.einsum(
        "k,kbcs->bcs", imag_part, swap_parts(basis), precision=highest
    )
    norm_square = lax.psum(jnp.sum(remainder * remainder), ("blk", "pair")) * mean_scale
    next_basis = remainder * lax.rsqrt(norm_square)
    return (dots, next_basis)


def solution(mesh):
    placed = (
        P(None, ("blk", "pair"), None, None),
        P(("blk", "pair"), None, None),
        P(),
        P(),
        P("blk", None, None),
        P("blk"),
    )
    return jax.shard_map(
        shards,
        mesh=mesh,
        in_specs=placed,
        out_specs=(P(), P(("blk", "pair"), None, None)),
        check_vma=False,
    )
```

profile of v0, /device:TPU:1, one launch (start us, length us, event | category | flops | bytes accessed | tf_op | source)
XLA Modules:
  0.0 644.9 jit_solution(5624039437728306315)
XLA Ops:
  9.1 14.2 %all_gather.3 = bf16[8,510,128]{2,1,0:T(8,128)(2,1)S(1)} all-gather(bf16[2,510,128]{2,1,0:T(8,128)(2,1)S(1)} %bitcast.112), channel_id=1, replica_groups=mesh['blk'=32,'pair'=4] {'pair'}, dimensions={0}, use_global_device_ids=true | all-gather | bytes 1305600 | tf_op jit(solution)/shard_map/all_gather | solution.py:72
  24.0 4.1 collective-permute-start.1
  28.0 3.1 collective-permute-start
  32.0 5.6 copy.56
  37.6 4.2 collective-permute-done.1
  45.3 3.4 broadcast_in_dim.35
  48.7 364.0 %while.12 = (s32[]{:T(128)}, f32[24,510,128]{2,1,0:T(8,128)}, s32[]{:T(128)}, s32[]{:T(128)}, s32[128,3]{1,0:T(8,128)S(1)}, /*index=5*/s32[]{:T(128)}, bf16[8,51...) while((s32[]{:T(128)}, f32[24,510,128]{2,1,0:T(8,128)}, ...), condition=%wide.region_3.4_spmd, body=%wide.region_0.3_spmd.sunk | while | flops 4272449536 | bytes 112527400 | solution.py:100
  49.8 5.1 gather_fusion.1
  54.8 21.3 %gather_fusion.2 = bf16[8,2,510,510]{3,1,2,0:T(2,128)(2,1)} fusion(bf16[8,2,510,510]{3,1,2,0:T(2,128)(2,1)} %get-tuple-element.299, s32[1024]{0:T(1024)S(1)} %pad_clamp_fusion.8), kind=kCustom, calls=%fused_computation.2.clone.1 | custom fusion | bytes 16646432 | tf_op jit(solution)/shard_map/while/body/gather | solution.py:92
  76.1 21.3 %copy.139 = bf16[8,2,510,510]{2,3,1,0:T(8,128)(2,1)} copy(bf16[8,2,510,510]{3,1,2,0:T(2,128)(2,1)} %gather_fusion.2) | data formatting | bytes 16646400 | tf_op jit(solution)/shard_map/while/body/gather | solution.py:92
  97.4 2.6 gather_fusion.3
  100.1 3.7 convolution_convert_fusion.4
  104.0 9.9 %convolution_select_fusion.4 = f32[8,510,128]{2,1,0:T(8,128)} fusion(bf16[8,510,510]{2,1,0:T(8,128)(2,1)} %gather_fusion.1, pred[8]{0:T(512)(128)(4,1)S(1)} %add_compare_fusion.2, bf16[8,2,510,510]{2,3,1,0:T(8,128)(2,1)} %copy.139, bf16[8,1,510,128]{2,3,0,1:T(8,128)(2,1)S(1)} %maximum_bitcast_fusion.5, bf16[8,1,510,128]{2,3,0,1:T(8,128)(2,1)S(1)} %bitcast.110), kind=kOutput, calls=%fused_computation.16.clone.1 | convolution fusion | flops 1600143360 | bytes 16662728 | tf_op jit(solution)/shard_map/while/body/pji,pjk->pik/dot_general | solution.py:60
  113.9 4.9 scatter_fusion
  118.7 2.6 gather_fusion.4
  121.4 3.7 convolution_convert_fusion.5
  125.3 9.5 %convolution_select_fusion.5 = f32[8,510,128]{2,1,0:T(8,128)} fusion(bf16[8,510,510]{2,1,0:T(8,128)(2,1)} %gather_fusion.1, pred[8]{0:T(512)(128)(4,1)S(1)} %add_compare_fusion.2, bf16[8,2,510,510]{2,3,1,0:T(8,128)(2,1)} %copy.139, bf16[8,1,510,128]{2,3,0,1:T(8,128)(2,1)S(1)} %maximum_bitcast_fusion.6, bf16[8,1,510,128]{2,3,0,1:T(8,128)(2,1)S(1)} %bitcast.109), kind=kOutput, calls=%fused_computation.15.clone.1 | convolution fusion | flops 1600143360 | bytes 16662728 | tf_op jit(solution)/shard_map/while/body/pji,pjk->pik/dot_general | solution.py:60
  134.8 4.9 scatter_fusion.1
  140.6 5.1 gather_fusion.1
  145.7 21.4 %gather_fusion.2 = bf16[8,2,510,510]{3,1,2,0:T(2,128)(2,1)} fusion(bf16[8,2,510,510]{3,1,2,0:T(2,128)(2,1)} %get-tuple-element.299, s32[1024]{0:T(1024)S(1)} %pad_clamp_fusion.8), kind=kCustom, calls=%fused_computation.2.clone.1 | custom fusion | bytes 16646432 | tf_op jit(solution)/shard_map/while/body/gather | solution.py:92
  167.1 21.3 %copy.139 = bf16[8,2,510,510]{2,3,1,0:T(8,128)(2,1)} copy(bf16[8,2,510,510]{3,1,2,0:T(2,128)(2,1)} %gather_fusion.2) | data formatting | bytes 16646400 | tf_op jit(solution)/shard_map/while/body/gather | solution.py:92
  188.4 2.6 gather_fusion.3
  191.0 3.7 convolution_convert_fusion.4
  194.9 9.9 %convolution_select_fusion.4 = f32[8,510,128]{2,1,0:T(8,128)} fusion(bf16[8,510,510]{2,1,0:T(8,128)(2,1)} %gather_fusion.1, pred[8]{0:T(512)(128)(4,1)S(1)} %add_compare_fusion.2, bf16[8,2,510,510]{2,3,1,0:T(8,128)(2,1)} %copy.139, bf16[8,1,510,128]{2,3,0,1:T(8,128)(2,1)S(1)} %maximum_bitcast_fusion.5, bf16[8,1,510,128]{2,3,0,1:T(8,128)(2,1)S(1)} %bitcast.110), kind=kOutput, calls=%fused_computation.16.clone.1 | convolution fusion | flops 1600143360 | bytes 16662728 | tf_op jit(solution)/shard_map/while/body/pji,pjk->pik/dot_general | solution.py:60
  204.8 4.9 scatter_fusion
  209.7 2.6 gather_fusion.4
  212.3 3.7 convolution_convert_fusion.5
  216.2 9.5 %convolution_select_fusion.5 = f32[8,510,128]{2,1,0:T(8,128)} fusion(bf16[8,510,510]{2,1,0:T(8,128)(2,1)} %gather_fusion.1, pred[8]{0:T(512)(128)(4,1)S(1)} %add_compare_fusion.2, bf16[8,2,510,510]{2,3,1,0:T(8,128)(2,1)} %copy.139, bf16[8,1,510,128]{2,3,0,1:T(8,128)(2,1)S(1)} %maximum_bitcast_fusion.6, bf16[8,1,510,128]{2,3,0,1:T(8,128)(2,1)S(1)} %bitcast.109), kind=kOutput, calls=%fused_computation.15.clone.1 | convolution fusion | flops 1600143360 | bytes 16662728 | tf_op jit(solution)/shard_map/while/body/pji,pjk->pik/dot_general | solution.py:60
  225.7 4.9 scatter_fusion.1
  231.6 5.1 gather_fusion.1
  236.7 21.2 %gather_fusion.2 = bf16[8,2,510,510]{3,1,2,0:T(2,128)(2,1)} fusion(bf16[8,2,510,510]{3,1,2,0:T(2,128)(2,1)} %get-tuple-element.299, s32[1024]{0:T(1024)S(1)} %pad_clamp_fusion.8), kind=kCustom, calls=%fused_computation.2.clone.1 | custom fusion | bytes 16646432 | tf_op jit(solution)/shard_map/while/body/gather | solution.py:92
  257.8 21.3 %copy.139 = bf16[8,2,510,510]{2,3,1,0:T(8,128)(2,1)} copy(bf16[8,2,510,510]{3,1,2,0:T(2,128)(2,1)} %gather_fusion.2) | data formatting | bytes 16646400 | tf_op jit(solution)/shard_map/while/body/gather | solution.py:92
  279.1 2.6 gather_fusion.3
  281.7 3.7 convolution_convert_fusion.4
  285.7 9.9 %convolution_select_fusion.4 = f32[8,510,128]{2,1,0:T(8,128)} fusion(bf16[8,510,510]{2,1,0:T(8,128)(2,1)} %gather_fusion.1, pred[8]{0:T(512)(128)(4,1)S(1)} %add_compare_fusion.2, bf16[8,2,510,510]{2,3,1,0:T(8,128)(2,1)} %copy.139, bf16[8,1,510,128]{2,3,0,1:T(8,128)(2,1)S(1)} %maximum_bitcast_fusion.5, bf16[8,1,510,128]{2,3,0,1:T(8,128)(2,1)S(1)} %bitcast.110), kind=kOutput, calls=%fused_computation.16.clone.1 | convolution fusion | flops 1600143360 | bytes 16662728 | tf_op jit(solution)/shard_map/while/body/pji,pjk->pik/dot_general | solution.py:60
  295.5 5.0 scatter_fusion
  300.5 2.6 gather_fusion.4
  303.1 3.7 convolution_convert_fusion.5
  307.1 9.5 %convolution_select_fusion.5 = f32[8,510,128]{2,1,0:T(8,128)} fusion(bf16[8,510,510]{2,1,0:T(8,128)(2,1)} %gather_fusion.1, pred[8]{0:T(512)(128)(4,1)S(1)} %add_compare_fusion.2, bf16[8,2,510,510]{2,3,1,0:T(8,128)(2,1)} %copy.139, bf16[8,1,510,128]{2,3,0,1:T(8,128)(2,1)S(1)} %maximum_bitcast_fusion.6, bf16[8,1,510,128]{2,3,0,1:T(8,128)(2,1)S(1)} %bitcast.109), kind=kOutput, calls=%fused_computation.15.clone.1 | convolution fusion | flops 1600143360 | bytes 16662728 | tf_op jit(solution)/shard_map/while/body/pji,pjk->pik/dot_general | solution.py:60
  316.5 4.9 scatter_fusion.1
  322.4 5.1 gather_fusion.1
  327.5 21.2 %gather_fusion.2 = bf16[8,2,510,510]{3,1,2,0:T(2,128)(2,1)} fusion(bf16[8,2,510,510]{3,1,2,0:T(2,128)(2,1)} %get-tuple-element.299, s32[1024]{0:T(1024)S(1)} %pad_clamp_fusion.8), kind=kCustom, calls=%fused_computation.2.clone.1 | custom fusion | bytes 16646432 | tf_op jit(solution)/shard_map/while/body/gather | solution.py:92
  348.7 21.3 %copy.139 = bf16[8,2,510,510]{2,3,1,0:T(8,128)(2,1)} copy(bf16[8,2,510,510]{3,1,2,0:T(2,128)(2,1)} %gather_fusion.2) | data formatting | bytes 16646400 | tf_op jit(solution)/shard_map/while/body/gather | solution.py:92
  370.0 2.6 gather_fusion.3
  372.6 3.7 convolution_convert_fusion.4
  376.5 9.9 %convolution_select_fusion.4 = f32[8,510,128]{2,1,0:T(8,128)} fusion(bf16[8,510,510]{2,1,0:T(8,128)(2,1)} %gather_fusion.1, pred[8]{0:T(512)(128)(4,1)S(1)} %add_compare_fusion.2, bf16[8,2,510,510]{2,3,1,0:T(8,128)(2,1)} %copy.139, bf16[8,1,510,128]{2,3,0,1:T(8,128)(2,1)S(1)} %maximum_bitcast_fusion.5, bf16[8,1,510,128]{2,3,0,1:T(8,128)(2,1)S(1)} %bitcast.110), kind=kOutput, calls=%fused_computation.16.clone.1 | convolution fusion | flops 1600143360 | bytes 16662728 | tf_op jit(solution)/shard_map/while/body/pji,pjk->pik/dot_general | solution.py:60
  386.4 4.9 scatter_fusion
  394.0 3.7 convolution_convert_fusion.5
  397.9 9.5 %convolution_select_fusion.5 = f32[8,510,128]{2,1,0:T(8,128)} fusion(bf16[8,510,510]{2,1,0:T(8,128)(2,1)} %gather_fusion.1, pred[8]{0:T(512)(128)(4,1)S(1)} %add_compare_fusion.2, bf16[8,2,510,510]{2,3,1,0:T(8,128)(2,1)} %copy.139, bf16[8,1,510,128]{2,3,0,1:T(8,128)(2,1)S(1)} %maximum_bitcast_fusion.6, bf16[8,1,510,128]{2,3,0,1:T(8,128)(2,1)S(1)} %bitcast.109), kind=kOutput, calls=%fused_computation.15.clone.1 | convolution fusion | flops 1600143360 | bytes 16662728 | tf_op jit(solution)/shard_map/while/body/pji,pjk->pik/dot_general | solution.py:60
  407.4 5.0 scatter_fusion.1
  412.7 3.4 convert.4
  416.3 4.9 collective-permute-start.3
  423.1 9.8 %collective-permute-done.3 = bf16[8,510,128]{2,1,0:T(8,128)(2,1)S(1)} collective-permute-done((bf16[8,510,128]{2,1,0:T(8,128)(2,1)S(1)}, bf16[8,510,128]{2,1,0:T(8,128)(2,1)S(1)}, u32[]{:S(2)}, u32[]{:S(2)}) %collective-permute-start.3) | collective-permute-done | bytes 1044512 | tf_op jit(solution)/shard_map/ppermute | solution.py:25
  432.9 4.4 collective-permute-done.2
  437.3 3.1 add_convert_fusion
  441.0 11.1 %slice_negate_fusion.2 = (f32[8,2,510,64]{3,1,2,0:T(2,128)}, f32[8,2,510,64]{3,1,2,0:T(2,128)}) fusion(f32[8,2,510,128]{3,1,2,0:T(2,128)} %param.8), kind=kLoop, calls=%fused_computation.39 | loop fusion | flops 522240 | bytes 8355840 | tf_op jit(solution)/shard_map/neg | solution.py:30
  452.1 15.8 %reduce-scatter.2.cloned.1.call-done = bf16[2,510,128]{2,1,0:T(8,128)(2,1)} async-done(((bf16[8,510,128]{2,1,0:T(8,128)(2,1)}), bf16[2,510,128]{2,1,0:T(8,128)(2,1)}) %reduce-scatter.2.cloned.1.call-update) | async-done | bytes 261136 | tf_op jit(solution)/shard_map/reduce_scatter | solution.py:106
  471.0 9.6 %fusion.33 = f32[1,8]{1,0:T(1,128)S(1)} fusion(f32[8,2,510,128]{3,1,2,0:T(2,128)S(1)} %copy-done, f32[2,510,128,1]{2,1,0,3:T(8,128)S(1)} %maximum_bitcast_fusion.2), kind=kOutput, calls=%fused_computation.51 | convolution fusion | flops 12533768 | bytes 4700192 | tf_op jit(solution)/shard_map/kbcs,bcs->k/dot_general | solution.py:113
  480.6 9.4 %fusion.24 = f32[1,8]{1,0:T(1,128)S(1)} fusion(f32[8,2,510,128]{3,1,2,0:T(2,128)S(1)} %copy-done, f32[2,510,128,1]{2,1,0,3:T(8,128)S(1)} %bitcast.111), kind=kOutput, calls=%fused_computation.48 | convolution fusion | flops 12533760 | bytes 4700192 | tf_op jit(solution)/shard_map/kbcs,bcs->k/dot_general | solution.py:112
  490.1 6.5 %pad_maximum_fusion.2 = f32[8,2,510,128]{3,1,2,0:T(2,128)} fusion(f32[8,2,510,64]{3,1,2,0:T(2,128)S(1)} %copy-done.3, f32[8,2,510,64]{3,1,2,0:T(2,128)S(1)} %copy-done.2), kind=kLoop, calls=%fused_computation.36 | loop fusion | flops 1044480 | bytes 8355840 | tf_op jit(solution)/shard_map/concatenate | solution.py:30
  496.6 66.1 %psum.14 = f32[2,8]{1,0:T(2,128)S(1)} all-reduce(f32[2,8]{1,0:T(2,128)S(1)} %pad_maximum_fusion.4), channel_id=1, replica_groups=mesh['blk'=32,'pair'=4] {'blk','pair'}, use_global_device_ids=true, to_apply=%region_5.6 | all-reduce | flops 16 | bytes 128 | tf_op jit(solution)/shard_map/psum | solution.py:114
  562.6 6.2 fusion.18
  568.8 3.7 fusion.16
  573.2 62.7 %psum.15 = f32[]{:T(128)} all-reduce(f32[]{:T(128)} %multiply_reduce_fusion), channel_id=1, replica_groups=mesh['blk'=32,'pair'=4] {'blk','pair'}, use_global_device_ids=true, to_apply=%region_7.8 | all-reduce | flops 1 | bytes 8 | tf_op jit(solution)/shard_map/psum | solution.py:120
  (86 shorter events, 22.1 us)
Async XLA Ops:
  7.2 24.7 %copy-start.8 = (s32[1,128,3]{1,0,2:T(1,128)S(1)}, s32[1,128,3]{1,0,2:T(1,128)}, u32[]{:S(2)}) copy-start(s32[1,128,3]{1,0,2:T(1,128)} %param.12) | copy-start | bytes 4612
  7.2 460.7 %reduce-scatter.2.cloned.1.call-start = ((), (), s32[]{:S(2)}) async-start(), calls=%async_computation.1 | async-start | bytes 1310720 | tf_op jit(solution)/shard_map/reduce_scatter | solution.py:106
  8.3 0.8 copy-start.4
  24.0 17.8 %collective-permute-start.1 = (bf16[8,510,128]{2,0,1:T(8,128)(2,1)S(1)}, bf16[8,510,128]{2,0,1:T(8,128)(2,1)}, u32[]{:S(2)}, u32[]{:S(2)}) collective-permute-start(bf16[8,510,128]{2,0,1:T(8,128)(2,1)S(1)} %copy.52), channel_id=1, source_target_pairs={{4,0},{8,4},{12,8},{16,12},{20,16},{24,20},{28,24},{32,28},{36,32}... | collective-permute-start | bytes 3133448 | tf_op jit(solution)/shard_map/ppermute | solution.py:17
  28.0 15.1 %collective-permute-start = (bf16[8,510,128]{2,0,1:T(8,128)(2,1)S(1)}, bf16[8,510,128]{2,0,1:T(8,128)(2,1)S(1)}, u32[]{:S(2)}, u32[]{:S(2)}) collective-permute-start(bf16[8,510,128]{2,0,1:T(8,128)(2,1)S(1)} %copy.52), channel_id=1, source_target_pairs={{0,4},{4,8},{8,12},{12,16},{16,20},{20,24},{24,28},{28,32},{32,36}... | collective-permute-start | bytes 3133448 | tf_op jit(solution)/shard_map/ppermute | solution.py:16
  416.3 24.1 %copy-start.6 = (f32[2,510,128]{2,0,1:T(2,128)S(1)}, f32[2,510,128]{2,0,1:T(2,128)}, u32[]{:S(2)}) copy-start(f32[2,510,128]{2,0,1:T(2,128)} %param.9) | copy-start | bytes 1566724
  416.3 16.6 %collective-permute-start.3 = (bf16[8,510,128]{2,1,0:T(8,128)(2,1)S(1)}, bf16[8,510,128]{2,1,0:T(8,128)(2,1)S(1)}, u32[]{:S(2)}, u32[]{:S(2)}) collective-permute-start(bf16[8,510,128]{2,1,0:T(8,128)(2,1)S(1)} %get-tuple-element.189), channel_id=1, source_target_pairs={{0,4},{4,8},{8,12},{12,16},{16,20},{20,24},{24,28},{28,32},{32,36}... | collective-permute-start | bytes 3133448 | tf_op jit(solution)/shard_map/ppermute | solution.py:25
  421.2 16.1 %collective-permute-start.2 = (bf16[8,510,128]{2,1,0:T(8,128)(2,1)S(1)}, bf16[8,510,128]{2,1,0:T(8,128)(2,1)S(1)}, u32[]{:S(2)}, u32[]{:S(2)}) collective-permute-start(bf16[8,510,128]{2,1,0:T(8,128)(2,1)S(1)} %get-tuple-element.188), channel_id=1, source_target_pairs={{4,0},{8,4},{12,8},{16,12},{20,16},{24,20},{28,24},{32,28},{36,32}... | collective-permute-start | bytes 3133448 | tf_op jit(solution)/shard_map/ppermute | solution.py:25
  452.1 17.0 %copy-start.5 = (f32[1,2,510,128]{3,1,2,0:T(2,128)S(1)}, f32[1,2,510,128]{3,1,2,0:T(2,128)}, u32[]{:S(2)}) copy-start(f32[1,2,510,128]{3,1,2,0:T(2,128)} %copy-done.4) | copy-start | bytes 1566724
  468.8 2.2 copy-start
  471.0 19.0 %copy-start.2 = (f32[8,2,510,64]{3,1,2,0:T(2,128)S(1)}, f32[8,2,510,64]{3,1,2,0:T(2,128)}, u32[]{:S(2)}) copy-start(f32[8,2,510,64]{3,1,2,0:T(2,128)} %get-tuple-element.186) | copy-start | bytes 6266884
  471.0 19.0 %copy-start.3 = (f32[8,2,510,64]{3,1,2,0:T(2,128)S(1)}, f32[8,2,510,64]{3,1,2,0:T(2,128)}, u32[]{:S(2)}) copy-start(f32[8,2,510,64]{3,1,2,0:T(2,128)} %get-tuple-element.187) | copy-start | bytes 6266884
  562.6 6.2 copy-start.1
  562.6 9.9 %copy-start.7 = (f32[2,8]{1,0:T(2,128)}, f32[2,8]{1,0:T(2,128)S(1)}, u32[]{:S(2)}) copy-start(f32[2,8]{1,0:T(2,128)S(1)} %broadcast_multiply_fusion.1) | copy-start | bytes 196
Sparse Core Ops, SparseCore 0:
  440.5 27.2 reduce-scatter.1
where the time goes:
time: 652 us; the launch traced here: 645 us
  local copies, waits for them, and re-layouts  230 us (35%)
  blocking collectives  143 us (22%)
  matrix products  136 us (21%)
  other arithmetic  71.2 us (11%)
  waiting for transfers between devices  34.2 us (5%)
  between operations  15.9 us (2%)
  starting transfers between devices  14 us (2%)
    gather x8, local copies, waits for them, and re-layouts, accumulate(): axial_pair = axial_table[table_rows]  170 us
    dot_general x8, matrix products, translate(): jnp.einsum('pji,pjk->pik', rotation, moved, preferred_element_type=jnp.fl...  77.4 us
    psum x1, blocking collectives, shards(): lax.psum(jnp.stack([real_local, imag_local]), ('blk', 'pair')) * mean_scale  66.1 us
    psum x1, blocking collectives, shards(): lax.psum(jnp.sum(remainder * remainder), ('blk', 'pair')) * mean_scale  62.7 us
    scatter-add x8, other arithmetic, accumulate(): return scattered.at[target_rows].add(forward).at[source_rows].add(backward)  39.4 us
    dot_general x8, matrix products, translate(): jnp.einsum('pij,pjk->pik', rotation, source, preferred_element_type=jnp.f...  29.5 us
    gather x4, local copies, waits for them, and re-layouts, accumulate(): rotation = rot_table[table_rows]  20.3 us
    reduce_scatter x1, waiting for transfers between devices, shards(): lax.psum_scatter(middle.astype(jnp.bfloat16), 'pair', scatter_dimension=0...  15.8 us
  transfers between devices with their start and end apart: 5, of which 4 were waited for; matrix products, arithmetic and copies ran while one was open for 3% of the time, Pallas kernels for 0%

commit v1 on v0

v1 whole, which is shorter than its diff:
```python
import functools

import jax
import jax.numpy as jnp
from jax import lax
from jax.experimental import pallas as pl
from jax.experimental.pallas import tpu as pltpu
from jax.sharding import PartitionSpec as P

MESH = pl.DeviceIdType.MESH
F32 = jnp.float32
BF16 = jnp.bfloat16
MODES = 510
PAD = 512
KRYLOV = 8
TABLES = 8
BLOCKS = 256
SPHERES = 64
ROWS = 16
CHUNKS = 4
MEAN_SCALE = 1.0 / (BLOCKS * MODES * 2 * SPHERES)

NT = (((1,), (1,)), ((), ()))
NN = (((1,), (0,)), ((), ()))


def dot(left, right, dims):
    return lax.dot_general(left, right, dims, preferred_element_type=F32)


def times_i(value):
    lane = lax.broadcasted_iota(jnp.int32, value.shape, 1)
    turned = pltpu.roll(value, SPHERES, axis=1)
    return jnp.where(lane < SPHERES, -turned, turned)


def fold(value):
    rows = value.shape[0]
    whole = rows // 8 * 8
    total = value[:8]
    for start in range(8, whole, 8):
        total = total + value[start : start + 8]
    if rows > whole:
        rest = value[whole:]
        total = total + jnp.concatenate([rest, jnp.zeros((8 - rest.shape[0], 128), F32)], axis=0)
    return total


def row_pieces(step):
    return [(start, min(step, MODES - start)) for start in range(0, MODES, step)]


def pair_rows(table, count):
    across = jnp.transpose(table)[:8]
    lane = lax.broadcasted_iota(jnp.int32, (8, 128), 1)
    row = lax.broadcasted_iota(jnp.int32, (8, 128), 0)
    return jnp.where((row == 2) & (lane >= count), -1.0, across)


def count_matrix(pairs, member):
    row = lax.broadcasted_iota(jnp.int32, (256, 128), 0)
    g_row = (row >> 5).astype(F32)
    back = ((row >> 4) & 1) == 1
    own = (2 * member + ((row >> 3) & 1)).astype(F32)
    column = (lax.broadcasted_iota(jnp.int32, (192, 128), 0) >> 3).astype(F32)
    total = None
    for off, back_here in ((1, False), (0, True), (1, True), (2, True)):
        a, b, g = (pairs[off][n : n + 1] for n in range(3))
        right_table = jnp.where(g_row == g, 1.0, 0.0)
        if back_here:
            hit = jnp.where(back & (own + 8.0 * (2 - off) == b), right_table, 0.0)
            place = jnp.where(column == a + 8.0 * off, 1.0, 0.0)
        else:
            hit = jnp.where((~back) & (own == a), right_table, 0.0)
            place = jnp.where(column == b, 1.0, 0.0)
        term = dot(hit.astype(BF16), place.astype(BF16), NT)
        total = term if total is None else total + term
    same = (lax.broadcasted_iota(jnp.int32, (256, 192), 0) & 7) == (
        lax.broadcasted_iota(jnp.int32, (256, 192), 1) & 7
    )
    return jnp.where(same, total, 0.0).astype(BF16)


def aggregate(counts, win, sums, group):
    halves = []
    for slab in (2 * group, 2 * group + 1):
        part = win[:, slab].reshape(12 * ROWS, PAD)
        halves.append(dot(counts, part, NN).reshape(32, 8, PAD))
    sums[group] = jnp.concatenate(halves, axis=1).astype(BF16)[:, :, :MODES]


def chain(g, groups, sums, rot, axial):
    half = len(groups) // 2
    parts = []
    for direction in range(2):
        for imag in range(2):
            for t in range(2):
                for n in groups[imag * half : imag * half + half]:
                    parts.append(sums[n, g * 4 + direction * 2 + t])
    rotation = rot[g]
    first, second = axial[g, 0], axial[g, 1]
    turned = dot(jnp.concatenate(parts, axis=0), rotation, NT).astype(BF16)
    count = turned.shape[0] // 2
    forward, backward = turned[:count], turned[count:]

    def swapped(value):
        return jnp.concatenate([-value[count // 2 :], value[: count // 2]], axis=0)

    moved = dot(forward, first, NT) + dot(swapped(forward), second, NT)
    moved = moved + dot(backward, first, NN) + dot(swapped(backward), second, NN)
    return dot(moved.astype(BF16), rotation, NN)


def field_of(groups, half, sums, rot, axial, field, acc):
    def step(g, carry):
        value = chain(g, groups, sums, rot, axial)
        acc[...] = jnp.where(g == 0, value, acc[...] + value)
        return carry

    lax.fori_loop(0, TABLES, step, 0)
    width = 8 * len(groups)
    for imag in range(2):
        for t in range(2):
            start = (imag * 2 + t) * width
            field[t, pl.ds(imag * 64 + half * 32, width), pl.ds(0, MODES)] = acc[pl.ds(start, width), :]


def kernel(
    basis_hbm, mie_hbm, rot_hbm, axial_hbm, table_hbm, count_ref,
    proj_ref, out_ref,
    basis, mie, rot, axial, table, wide, current, pairs, win, sums, acc, field, image, red_a, red_b,
    load_sem, send_sem, recv_sem, pair_send, pair_recv, a_send, a_recv, b_send, b_recv,
):
    blk_ways, pair_ways = lax.axis_size("blk"), lax.axis_size("pair")
    blk, member = lax.axis_index("blk"), lax.axis_index("pair")
    core = lax.rem(blk, 2)
    row = blk // 2
    row_ways = blk_ways // 2
    inner = blk + 1 - 2 * core
    outer = lax.rem(blk - 1 + 2 * core + blk_ways, blk_ways)
    right, left, far = (lax.rem(member + n, pair_ways) for n in (1, 3, 2))

    last = KRYLOV - 1
    loads = [
        pltpu.make_async_copy(basis_hbm.at[last], basis.at[last], load_sem.at[0]),
        pltpu.make_async_copy(table_hbm.at[0], table, load_sem.at[1]),
        pltpu.make_async_copy(basis_hbm.at[pl.ds(0, last)], basis.at[pl.ds(0, last)], load_sem.at[2]),
        pltpu.make_async_copy(mie_hbm, mie, load_sem.at[3]),
        pltpu.make_async_copy(rot_hbm, rot, load_sem.at[4]),
        pltpu.make_async_copy(axial_hbm, axial, load_sem.at[5]),
    ]
    for load in loads:
        load.start()

    spot = core * pair_ways + member
    group_a = []
    for n in range(1, 2 * pair_ways):
        other = lax.rem(spot + n, 2 * pair_ways)
        group_a.append((other, (2 * row + other // pair_ways, lax.rem(other, pair_ways))))
    group_b = []
    for n in range(1, row_ways):
        other = lax.rem(row + n, row_ways)
        group_b.append((other, (2 * other + core, member)))
    barrier = pltpu.get_barrier_semaphore()
    for device in [(outer, member)] + [d for _, d in group_a] + [d for _, d in group_b]:
        pl.semaphore_signal(barrier, inc=1, device_id=device, device_id_type=MESH)

    loads[0].wait()
    current[:, pl.ds(MODES - 6, 8), :] = jnp.zeros((2, 8, 128), F32)
    mine = 4 + member
    for t in range(2):
        current[t, pl.ds(0, MODES), :] = basis[last, t]
    flipped = [jnp.transpose(current[t]) for t in range(2)]
    for slab in range(16):
        half, imag, q = slab // 8, slab // 4 % 2, slab % 4
        start = imag * 64 + half * 32 + q * 8
        both = jnp.concatenate([value[start : start + 8] for value in flipped], axis=0)
        win[mine, slab] = both.astype(BF16)
    pl.semaphore_wait(barrier, 1 + len(group_a) + len(group_b))

    width = 16 // CHUNKS
    sends = []

    def send(source_slot, target_slot, chunk, device):
        place = pl.ds(chunk * width, width)
        copy = pltpu.make_async_remote_copy(
            src_ref=win.at[source_slot, place],
            dst_ref=win.at[target_slot, place],
            send_sem=send_sem.at[len(sends)],
            recv_sem=recv_sem.at[target_slot * CHUNKS + chunk],
            device_id=device,
            device_id_type=MESH,
        )
        copy.start()
        sends.append(copy)

    def arrived(slot, chunk):
        place = pl.ds(chunk * width, width)
        pltpu.make_async_remote_copy(
            src_ref=win.at[slot, place],
            dst_ref=win.at[slot, place],
            send_sem=send_sem.at[0],
            recv_sem=recv_sem.at[slot * CHUNKS + chunk],
            device_id=(inner, member),
            device_id_type=MESH,
        ).wait_recv()

    to_inner, to_outer = 8 * core, 8 * (1 - core)
    from_inner, from_outer = 8 * (1 - core), 8 * core
    for chunk in range(CHUNKS):
        send(mine, to_outer + member, chunk, (outer, member))
        send(mine, mine, chunk, (blk, right))
        send(mine, mine, chunk, (blk, left))
        send(mine, to_inner + member, chunk, (inner, member))

    loads[1].wait()
    wide[...] = jnp.zeros((128, 128), F32)
    wide[:, pl.ds(0, 3)] = table[...].astype(F32)
    pairs[1] = pair_rows(wide[...], count_ref[0])
    pair_copies = []
    for n, (slot, device) in enumerate(((2 * core, (inner, member)), (2 - 2 * core, (outer, member)))):
        copy = pltpu.make_async_remote_copy(
            src_ref=pairs.at[1],
            dst_ref=pairs.at[slot],
            send_sem=pair_send.at[n],
            recv_sem=pair_recv.at[n],
            device_id=device,
            device_id_type=MESH,
        )
        copy.start()
        pair_copies.append(copy)

    def forward(chunk):
        for origin, keep_on, device in ((left, 0, right), (right, 1, left)):
            arrived(4 + origin, chunk)
            send(4 + origin, to_outer + origin, chunk, (outer, member))
            if chunk % 2 == keep_on:
                send(4 + origin, 4 + origin, chunk, (blk, device))
            send(4 + origin, to_inner + origin, chunk, (inner, member))

    def forward_far(chunk):
        arrived(4 + far, chunk)
        send(4 + far, to_outer + far, chunk, (outer, member))
        send(4 + far, to_inner + far, chunk, (inner, member))

    def landed(chunks):
        for chunk in chunks:
            for n in range(pair_ways):
                arrived(from_inner + n, chunk)
                arrived(from_outer + n, chunk)

    forward(0)
    forward(1)
    forward_far(0)
    forward(2)
    forward_far(1)
    forward(3)
    forward_far(2)
    forward_far(3)
    for copy in pair_copies:
        copy.wait()
    counts = count_matrix([pairs[n] for n in range(3)], member)
    loads[4].wait()
    loads[5].wait()
    landed(range(CHUNKS))
    for group in range(8):
        aggregate(counts, win, sums, group)
    for half in range(2):
        groups = list(range(4 * half, 4 * half + 4))
        field_of(groups, half, sums, rot, axial, field, acc)

    loads[2].wait()
    loads[3].wait()
    real = [jnp.zeros((8, 128), F32)] * KRYLOV
    imag = [jnp.zeros((8, 128), F32)] * KRYLOV
    for t in range(2):
        upright = jnp.transpose(field[t])
        for start, size in row_pieces(64):
            place = pl.ds(start, size)
            here = upright[start : start + size]
            scale = mie[t, place, :]
            lane = lax.broadcasted_iota(jnp.int32, scale.shape, 1)
            other = pltpu.roll(scale, SPHERES, axis=1)
            scale_real = jnp.where(lane < SPHERES, scale, other)
            scale_imag = jnp.where(lane < SPHERES, other, scale)
            value = basis[last, t, place, :] - (scale_real * here + scale_imag * times_i(here))
            image[t, place, :] = value
            turned = times_i(value)
            for k in range(KRYLOV):
                vector = basis[k, t, place, :]
                real[k] = real[k] + fold(vector * value)
                imag[k] = imag[k] - fold(vector * turned)

    def tile_of(parts):
        rows = [jnp.sum(part, axis=0, keepdims=True) for part in parts]
        return jnp.sum(jnp.concatenate(rows, axis=0), axis=1, keepdims=True)

    def all_sum(call, value):
        steps = ((red_a, a_send, a_recv, group_a, spot), (red_b, b_send, b_recv, group_b, row))
        for store, send_sems, recv_sems, group, index in steps:
            store[call, index] = value
            copies = []
            for n, (other, device) in enumerate(group):
                copy = pltpu.make_async_remote_copy(
                    src_ref=store.at[call, index],
                    dst_ref=store.at[call, index],
                    send_sem=send_sems.at[call, n],
                    recv_sem=recv_sems.at[call, index],
                    device_id=device,
                    device_id_type=MESH,
                )
                copy.start()
                copies.append(copy)
            for other, device in group:
                pltpu.make_async_remote_copy(
                    src_ref=store.at[call, other],
                    dst_ref=store.at[call, other],
                    send_sem=send_sems.at[call, 0],
                    recv_sem=recv_sems.at[call, other],
                    device_id=device,
                    device_id_type=MESH,
                ).wait_recv()
            value = store[call, 0]
            for n in range(1, len(group) + 1):
                value = value + store[call, n]
            for copy in copies:
                copy.wait_send()
        return value

    lane = lax.broadcasted_iota(jnp.int32, (8, 128), 1)
    packed = jnp.where(lane == 0, tile_of(real), jnp.where(lane == 1, tile_of(imag), 0.0))
    dots = all_sum(0, packed) * MEAN_SCALE
    proj_ref[...] = jnp.transpose(dots)[:2]
    for copy in sends:
        copy.wait_send()

    square = jnp.zeros((8, 128), F32)
    for t in range(2):
        for start, size in row_pieces(64):
            place = pl.ds(start, size)
            plain = image[t, place, :]
            turned = jnp.zeros((size, 128), F32)
            for k in range(KRYLOV):
                vector = basis[k, t, place, :]
                plain = plain - dots[k : k + 1, 0:1] * vector
                turned = turned + dots[k : k + 1, 1:2] * vector
            value = plain - times_i(turned)
            image[t, place, :] = value
            square = square + fold(value * value)
    norm_square = jnp.sum(all_sum(1, square)) * MEAN_SCALE
    scale = lax.rsqrt(jnp.full((8, 128), norm_square, F32))[:1]
    for t in range(2):
        out_ref[t] = image[t] * scale


def shards(basis, mie_coeffs, rot_table, axial_table, pair_table, pair_count):
    blocks = basis.shape[1]
    anywhere = pl.BlockSpec(memory_space=pl.ANY)
    return pl.pallas_call(
        kernel,
        out_shape=(
            jax.ShapeDtypeStruct((2, KRYLOV), F32),
            jax.ShapeDtypeStruct((blocks, MODES, 2 * SPHERES), F32),
        ),
        in_specs=[anywhere] * 5 + [pl.BlockSpec(memory_space=pltpu.SMEM)],
        out_specs=(pl.BlockSpec(memory_space=pltpu.VMEM),) * 2,
        scratch_shapes=[
            pltpu.VMEM((KRYLOV, 2, MODES, 128), F32),
            pltpu.VMEM((2, MODES, 128), F32),
            pltpu.VMEM((TABLES, MODES, MODES), BF16),
            pltpu.VMEM((TABLES, 2, MODES, MODES), BF16),
            pltpu.VMEM((128, 3), jnp.int32),
            pltpu.VMEM((128, 128), F32),
            pltpu.VMEM((2, PAD, 128), F32),
            pltpu.VMEM((3, 8, 128), F32),
            pltpu.VMEM((12, 16, ROWS, PAD), BF16),
            pltpu.VMEM((8, 32, ROWS, MODES), BF16),
            pltpu.VMEM((128, MODES), F32),
            pltpu.VMEM((2, 128, PAD), F32),
            pltpu.VMEM((2, MODES, 128), F32),
            pltpu.VMEM((2, 8, 8, 128), F32),
            pltpu.VMEM((2, 16, 8, 128), F32),
            pltpu.SemaphoreType.DMA((6,)),
            pltpu.SemaphoreType.DMA((11 * CHUNKS,)),
            pltpu.SemaphoreType.DMA((12 * CHUNKS,)),
            pltpu.SemaphoreType.DMA((2,)),
            pltpu.SemaphoreType.DMA((2,)),
            pltpu.SemaphoreType.DMA((2, 7)),
            pltpu.SemaphoreType.DMA((2, 8)),
            pltpu.SemaphoreType.DMA((2, 15)),
            pltpu.SemaphoreType.DMA((2, 16)),
        ],
        compiler_params=pltpu.CompilerParams(
            collective_id=0, has_side_effects=True, vmem_limit_bytes=56 * 1024 * 1024
        ),
        name="arnoldi",
    )(basis, mie_coeffs, rot_table, axial_table, pair_table, pair_count)


def solution(mesh):
    placed = (
        P(None, ("blk", "pair"), None, None),
        P(("blk", "pair"), None, None),
        P(),
        P(),
        P("blk", None, None),
        P("blk"),
    )
    return jax.shard_map(
        shards,
        mesh=mesh,
        in_specs=placed,
        out_specs=(P(), P(("blk", "pair"), None, None)),
        check_vma=False,
    )
```

time: 652 us -> 89.3 us (0.14); the launches traced: 645 us -> 88.8 us
  local copies, waits for them, and re-layouts: 230 us -> 23.2 us
  blocking collectives: 143 us -> 0 us
  matrix products: 136 us -> 0 us
  other arithmetic: 71.2 us -> 0 us
  Pallas kernels: 0 us -> 64.3 us
  waiting for transfers between devices: 34.2 us -> 0 us
  between operations: 15.9 us -> 1.29 us
  starting transfers between devices: 14 us -> 0 us
    gather x24 -> x0, local copies, waits for them, and re-layouts: 214 us -> none  [the longest x8 170 us: accumulate(): axial_pair = axial_table[table_rows]]
    dot_general x20 -> x0, matrix products: 136 us -> none  [the longest x8 77.4 us: translate(): jnp.einsum('pji,pjk->pik', rotation, moved, preferred_element_type=jnp.fl...]
    psum x2 -> x0, blocking collectives: 129 us -> none  [the longest x1 66.1 us: shards(): lax.psum(jnp.stack([real_local, imag_local]), ('blk', 'pair')) * mean_scale]
    pallas_call x0 -> x1, Pallas kernels: none -> 64.3 us  [shards(): pl.pallas_call(kernel, out_shape=(jax.ShapeDtypeStruct((2, KRYLOV), F32),...]
    scatter-add x8 -> x0, other arithmetic: 39.4 us -> none  [accumulate(): return scattered.at[target_rows].add(forward).at[source_rows].add(backward)]
    ppermute x4 -> x0, waiting for transfers between devices: 18.4 us -> none  [the longest x2 14.2 us: shifted(): lax.ppermute(value, axis, [(source, source + steps) for source in range(l...]
    unnamed x21 -> x8, local copies, waits for them, and re-layouts: 3.38 us -> 20.9 us
    reduce_scatter x1 -> x0, waiting for transfers between devices: 15.8 us -> none  [shards(): lax.psum_scatter(middle.astype(jnp.bfloat16), 'pair', scatter_dimension=0...]
  transfers between devices with their start and end apart: 5 -> 0, of which waited for: 4 -> 0; matrix products, arithmetic and copies ran while one was open for 3% -> 0% of each run, Pallas kernels for 0% -> 0%
where the time goes in v1:
time: 89.3 us; the launch traced here: 88.8 us
  Pallas kernels  64.3 us (72%)
  local copies, waits for them, and re-layouts  23.2 us (26%)
  between operations  1.29 us (1%)
    pallas_call x1, Pallas kernels, shards(): pl.pallas_call(kernel, out_shape=(jax.ShapeDtypeStruct((2, KRYLOV), F32),...  64.3 us
    unnamed x8, local copies, waits for them, and re-layouts  20.9 us
    pallas_call x1, local copies, waits for them, and re-layouts, shards(): pl.pallas_call(kernel, out_shape=(jax.ShapeDtypeStruct((2, KRYLOV), F32),...  2.23 us

profile of v1, /device:TPU:1, one launch (start us, length us, event | category | flops | bytes accessed | tf_op | source)
XLA Modules:
  0.0 88.8 jit_solution(10684539556138415300)
XLA Ops:
  1.3 1.4 %copy.12.table_hbm = s32[1,128,3]{2,1,0:T(8,128)} copy(s32[1,128,3]{1,0,2:T(1,128)} %param.10) | data formatting | bytes 3072 | tf_op args[4]
  2.7 1.9 %copy.9.mie_hbm = f32[2,510,128]{2,1,0:T(8,128)} copy(f32[2,510,128]{2,0,1:T(2,128)} %param.7) | data formatting | bytes 1044480 | tf_op args[1]
  4.5 0.0 copy-start
  4.6 4.8 %copy.8.basis_hbm = f32[8,2,510,128]{3,2,1,0:T(8,128)} copy(f32[8,2,510,128]{3,1,2,0:T(2,128)} %param.6) | data formatting | bytes 8355840 | tf_op args[0]
  9.3 0.0 copy-done
  9.3 3.4 %copy.10.rot_hbm = bf16[8,510,510]{2,1,0:T(8,128)(2,1)} copy(bf16[8,510,510]{2,0,1:T(8,128)(2,1)S(1)} %copy-done) | data formatting | bytes 8323200 | tf_op args[2]
  12.7 8.3 %copy.11.axial_hbm = bf16[8,2,510,510]{3,2,1,0:T(8,128)(2,1)} copy(bf16[8,2,510,510]{3,1,2,0:T(2,128)(2,1)} %param.9) | data formatting | bytes 16646400 | tf_op args[3]
  21.0 64.3 %arnoldi.1 = (f32[2,8]{1,0:T(2,128)}, f32[2,510,128]{2,1,0:T(8,128)}) custom-call(f32[8,2,510,128]{3,2,1,0:T(8,128)} %copy.8.basis_hbm, f32[2,510,128]{2,1,0:T(8,128)} %copy.9.mie_hbm, bf16[8,510,510]{2,1,0:T(8,128)(2,1)} %copy.10.rot_hbm, bf16[8,2,510,510]{3,2,1,0:T(8,128)(2,1)} %copy.11.axial_hbm, s32[1,128,3]{2,1,0:T(8,128)} %copy.12.table_hbm, ...), custom_call_target="tpu_custom_call" | custom-call | tf_op jit(solution)/shard_map/arnoldi/pallas_call | solution.py:359
  85.3 2.2 %copy.13 = f32[2,510,128]{2,0,1:T(2,128)} copy(f32[2,510,128]{2,1,0:T(8,128)} %get-tuple-element.3) | data formatting | bytes 1044480 | tf_op jit(solution)/shard_map/arnoldi/pallas_call | solution.py:359
  87.5 1.2 %copy.16 = f32[2,8]{1,0:T(2,128)} copy(f32[2,8]{1,0:T(2,128)} %get-tuple-element.6) | data formatting | bytes 128
Async XLA Ops:
  4.5 4.8 %copy-start = (bf16[8,510,510]{2,0,1:T(8,128)(2,1)S(1)}, bf16[8,510,510]{2,0,1:T(8,128)(2,1)}, u32[]{:S(2)}) copy-start(bf16[8,510,510]{2,0,1:T(8,128)(2,1)} %param.8) | copy-start | bytes 12484804

commit v2 on v1

--- a/solution.py
+++ b/solution.py
@@ -46,15 +46,8 @@
     return total
 
 
-def row_pieces(step):
-    return [(start, min(step, MODES - start)) for start in range(0, MODES, step)]
-
-
-def pair_rows(table, count):
-    across = jnp.transpose(table)[:8]
-    lane = lax.broadcasted_iota(jnp.int32, (8, 128), 1)
-    row = lax.broadcasted_iota(jnp.int32, (8, 128), 0)
-    return jnp.where((row == 2) & (lane >= count), -1.0, across)
+def row_pieces(step, total):
+    return [(start, min(step, total - start)) for start in range(0, total, step)]
 
 
 def count_matrix(pairs, member):
@@ -65,7 +58,7 @@
     column = (lax.broadcasted_iota(jnp.int32, (192, 128), 0) >> 3).astype(F32)
     total = None
     for off, back_here in ((1, False), (0, True), (1, True), (2, True)):
-        a, b, g = (pairs[off][n : n + 1] for n in range(3))
+        a, b, g = (pairs[off, n : n + 1, :] for n in range(3))
         right_table = jnp.where(g_row == g, 1.0, 0.0)
         if back_here:
             hit = jnp.where(back & (own + 8.0 * (2 - off) == b), right_table, 0.0)
@@ -86,7 +79,7 @@
     for slab in (2 * group, 2 * group + 1):
         part = win[:, slab].reshape(12 * ROWS, PAD)
         halves.append(dot(counts, part, NN).reshape(32, 8, PAD))
-    sums[group] = jnp.concatenate(halves, axis=1).astype(BF16)[:, :, :MODES]
+    sums[group] = jnp.concatenate(halves, axis=1).astype(BF16)
 
 
 def chain(g, groups, sums, rot, axial):
@@ -111,24 +104,22 @@
     return dot(moved.astype(BF16), rotation, NN)
 
 
-def field_of(groups, half, sums, rot, axial, field, acc):
-    def step(g, carry):
+def field_of(sums, rot, axial, field):
+    groups = [half * 4 + imag * 2 + n for imag in range(2) for half in range(2) for n in range(2)]
+    total = None
+    for g in range(TABLES):
         value = chain(g, groups, sums, rot, axial)
-        acc[...] = jnp.where(g == 0, value, acc[...] + value)
-        return carry
-
-    lax.fori_loop(0, TABLES, step, 0)
-    width = 8 * len(groups)
+        total = value if total is None else total + value
     for imag in range(2):
         for t in range(2):
-            start = (imag * 2 + t) * width
-            field[t, pl.ds(imag * 64 + half * 32, width), pl.ds(0, MODES)] = acc[pl.ds(start, width), :]
+            start = (imag * 2 + t) * 64
+            field[t, imag * 64 : imag * 64 + 64] = total[start : start + 64]
 
 
 def kernel(
     basis_hbm, mie_hbm, rot_hbm, axial_hbm, table_hbm, count_ref,
     proj_ref, out_ref,
-    basis, mie, rot, axial, table, wide, current, pairs, win, sums, acc, field, image, red_a, red_b,
+    basis, mie_raw, mie, rot_raw, axial_raw, rot, axial, table, current, pairs, win, sums, field, mixed, image, red_a, red_b,
     load_sem, send_sem, recv_sem, pair_send, pair_recv, a_send, a_recv, b_send, b_recv,
 ):
     blk_ways, pair_ways = lax.axis_size("blk"), lax.axis_size("pair")
@@ -141,15 +132,18 @@
     right, left, far = (lax.rem(member + n, pair_ways) for n in (1, 3, 2))
 
     last = KRYLOV - 1
-    loads = [
-        pltpu.make_async_copy(basis_hbm.at[last], basis.at[last], load_sem.at[0]),
-        pltpu.make_async_copy(table_hbm.at[0], table, load_sem.at[1]),
-        pltpu.make_async_copy(basis_hbm.at[pl.ds(0, last)], basis.at[pl.ds(0, last)], load_sem.at[2]),
-        pltpu.make_async_copy(mie_hbm, mie, load_sem.at[3]),
-        pltpu.make_async_copy(rot_hbm, rot, load_sem.at[4]),
-        pltpu.make_async_copy(axial_hbm, axial, load_sem.at[5]),
+    rows = 2 * MODES
+    first_rows = last * rows // 8 * 8
+    head, tail = pl.ds(0, first_rows), pl.ds(first_rows, KRYLOV * rows - first_rows)
+    load_last = pltpu.make_async_copy(basis_hbm.at[tail], basis.at[tail], load_sem.at[0])
+    load_table = pltpu.make_async_copy(table_hbm, table, load_sem.at[1])
+    load_rot = pltpu.make_async_copy(rot_hbm, rot_raw, load_sem.at[2])
+    load_axial = [
+        pltpu.make_async_copy(axial_hbm.at[g], axial_raw.at[g], load_sem.at[5 + g]) for g in range(TABLES)
     ]
-    for load in loads:
+    load_rest = pltpu.make_async_copy(basis_hbm.at[head], basis.at[head], load_sem.at[3])
+    load_mie = pltpu.make_async_copy(mie_hbm, mie_raw, load_sem.at[4])
+    for load in [load_last, load_table, load_rot, *load_axial, load_rest, load_mie]:
         load.start()
 
     spot = core * pair_ways + member
@@ -165,11 +159,11 @@
     for device in [(outer, member)] + [d for _, d in group_a] + [d for _, d in group_b]:
         pl.semaphore_signal(barrier, inc=1, device_id=device, device_id_type=MESH)
 
-    loads[0].wait()
+    load_last.wait()
     current[:, pl.ds(MODES - 6, 8), :] = jnp.zeros((2, 8, 128), F32)
     mine = 4 + member
     for t in range(2):
-        current[t, pl.ds(0, MODES), :] = basis[last, t]
+        current[t, pl.ds(0, MODES), :] = basis[pl.ds(last * rows + t, MODES, stride=2), :]
     flipped = [jnp.transpose(current[t]) for t in range(2)]
     for slab in range(16):
         half, imag, q = slab // 8, slab // 4 % 2, slab % 4
@@ -213,10 +207,12 @@
         send(mine, mine, chunk, (blk, left))
         send(mine, to_inner + member, chunk, (inner, member))
 
-    loads[1].wait()
-    wide[...] = jnp.zeros((128, 128), F32)
-    wide[:, pl.ds(0, 3)] = table[...].astype(F32)
-    pairs[1] = pair_rows(wide[...], count_ref[0])
+    load_table.wait()
+    live = lax.broadcasted_iota(jnp.int32, (1, 128), 1) < count_ref[0]
+    pairs[1, pl.ds(0, 1), :] = table[0].astype(F32)
+    pairs[1, pl.ds(1, 1), :] = table[1].astype(F32)
+    pairs[1, pl.ds(2, 1), :] = jnp.where(live, table[2].astype(F32), -1.0)
+    pairs[1, pl.ds(3, 5), :] = jnp.zeros((5, 128), F32)
     pair_copies = []
     for n, (slot, device) in enumerate(((2 * core, (inner, member)), (2 - 2 * core, (outer, member)))):
         copy = pltpu.make_async_remote_copy(
@@ -249,47 +245,74 @@
                 arrived(from_inner + n, chunk)
                 arrived(from_outer + n, chunk)
 
+    rot[:, pl.ds(PAD - 16, 16), :] = jnp.zeros((TABLES, 16, PAD), BF16)
+    rot[:, :, pl.ds(PAD - 128, 128)] = jnp.zeros((TABLES, PAD, 128), BF16)
+
+    def order_rot():
+        load_rot.wait()
+        for start, size in row_pieces(32, MODES):
+            value = rot_raw[pl.ds(start, size)]
+            rot[:, pl.ds(start, size), pl.ds(0, MODES)] = jnp.swapaxes(value, 0, 1)
+
+    def order_axial(g):
+        load_axial[g].wait()
+        axial[g, :, pl.ds(PAD - 16, 16), :] = jnp.zeros((2, 16, PAD), BF16)
+        axial[g, :, :, pl.ds(PAD - 128, 128)] = jnp.zeros((2, PAD, 128), BF16)
+        for start, size in row_pieces(64, MODES):
+            value = axial_raw[g, pl.ds(start, size)]
+            axial[g, :, pl.ds(start, size), pl.ds(0, MODES)] = jnp.swapaxes(value, 0, 1)
+
+    def order_mie():
+        load_mie.wait()
+        for start, size in row_pieces(32, MODES):
+            scale = mie_raw[pl.ds(start, size)].reshape(2 * size, 128)
+            lane = lax.broadcasted_iota(jnp.int32, scale.shape, 1)
+            other = pltpu.roll(scale, SPHERES, axis=1)
+            mie[0, pl.ds(2 * start, 2 * size), :] = jnp.where(lane < SPHERES, scale, other)
+            mie[1, pl.ds(2 * start, 2 * size), :] = jnp.where(lane < SPHERES, other, scale)
+
+    order_rot()
     forward(0)
+    order_axial(0)
+    order_axial(1)
     forward(1)
     forward_far(0)
+    order_axial(2)
+    order_axial(3)
     forward(2)
     forward_far(1)
+    order_axial(4)
+    order_axial(5)
     forward(3)
     forward_far(2)
-    forward_far(3)
+    order_axial(6)
+    order_axial(7)
     for copy in pair_copies:
         copy.wait()
-    counts = count_matrix([pairs[n] for n in range(3)], member)
-    loads[4].wait()
-    loads[5].wait()
+    counts = count_matrix(pairs, member)
+    order_mie()
+    forward_far(3)
     landed(range(CHUNKS))
     for group in range(8):
         aggregate(counts, win, sums, group)
-    for half in range(2):
-        groups = list(range(4 * half, 4 * half + 4))
-        field_of(groups, half, sums, rot, axial, field, acc)
-
-    loads[2].wait()
-    loads[3].wait()
+    field_of(sums, rot, axial, field)
+
+    load_rest.wait()
     real = [jnp.zeros((8, 128), F32)] * KRYLOV
     imag = [jnp.zeros((8, 128), F32)] * KRYLOV
     for t in range(2):
-        upright = jnp.transpose(field[t])
-        for start, size in row_pieces(64):
-            place = pl.ds(start, size)
-            here = upright[start : start + size]
-            scale = mie[t, place, :]
-            lane = lax.broadcasted_iota(jnp.int32, scale.shape, 1)
-            other = pltpu.roll(scale, SPHERES, axis=1)
-            scale_real = jnp.where(lane < SPHERES, scale, other)
-            scale_imag = jnp.where(lane < SPHERES, other, scale)
-            value = basis[last, t, place, :] - (scale_real * here + scale_imag * times_i(here))
-            image[t, place, :] = value
-            turned = times_i(value)
-            for k in range(KRYLOV):
-                vector = basis[k, t, place, :]
-                real[k] = real[k] + fold(vector * value)
-                imag[k] = imag[k] - fold(vector * turned)
+        mixed[pl.ds(t, PAD, stride=2), :] = jnp.transpose(field[t])
+    for start, size in row_pieces(64, rows):
+        place = pl.ds(start, size)
+        here = mixed[place, :]
+        product = mie[0, place, :] * here + mie[1, place, :] * times_i(here)
+        value = basis[pl.ds(last * rows + start, size), :] - product
+        image[place, :] = value
+        turned = times_i(value)
+        for k in range(KRYLOV):
+            vector = basis[pl.ds(k * rows + start, size), :]
+            real[k] = real[k] + fold(vector * value)
+            imag[k] = imag[k] - fold(vector * turned)
 
     def tile_of(parts):
         rows = [jnp.sum(part, axis=0, keepdims=True) for part in parts]
@@ -323,64 +346,63 @@
             value = store[call, 0]
             for n in range(1, len(group) + 1):
                 value = value + store[call, n]
-            for copy in copies:
-                copy.wait_send()
+            sends.extend(copies)
         return value
 
     lane = lax.broadcasted_iota(jnp.int32, (8, 128), 1)
     packed = jnp.where(lane == 0, tile_of(real), jnp.where(lane == 1, tile_of(imag), 0.0))
     dots = all_sum(0, packed) * MEAN_SCALE
     proj_ref[...] = jnp.transpose(dots)[:2]
+
+    square = jnp.zeros((8, 128), F32)
+    for start, size in row_pieces(64, rows):
+        place = pl.ds(start, size)
+        plain = image[place, :]
+        turned = jnp.zeros((size, 128), F32)
+        for k in range(KRYLOV):
+            vector = basis[pl.ds(k * rows + start, size), :]
+            plain = plain - dots[k : k + 1, 0:1] * vector
+            turned = turned + dots[k : k + 1, 1:2] * vector
+        value = plain - times_i(turned)
+        image[place, :] = value
+        square = square + fold(value * value)
+    norm_square = jnp.sum(all_sum(1, square)) * MEAN_SCALE
+    scale = lax.rsqrt(jnp.full((8, 128), norm_square, F32))[:1]
+    out_ref[...] = image[...] * scale
     for copy in sends:
         copy.wait_send()
 
-    square = jnp.zeros((8, 128), F32)
-    for t in range(2):
-        for start, size in row_pieces(64):
-            place = pl.ds(start, size)
-            plain = image[t, place, :]
-            turned = jnp.zeros((size, 128), F32)
-            for k in range(KRYLOV):
-                vector = basis[k, t, place, :]
-                plain = plain - dots[k : k + 1, 0:1] * vector
-                turned = turned + dots[k : k + 1, 1:2] * vector
-            value = plain - times_i(turned)
-            image[t, place, :] = value
-            square = square + fold(value * value)
-    norm_square = jnp.sum(all_sum(1, square)) * MEAN_SCALE
-    scale = lax.rsqrt(jnp.full((8, 128), norm_square, F32))[:1]
-    for t in range(2):
-        out_ref[t] = image[t] * scale
-
 
 def shards(basis, mie_coeffs, rot_table, axial_table, pair_table, pair_count):
-    blocks = basis.shape[1]
+    rows = 2 * MODES
     anywhere = pl.BlockSpec(memory_space=pl.ANY)
-    return pl.pallas_call(
+    dots, vector = pl.pallas_call(
         kernel,
         out_shape=(
             jax.ShapeDtypeStruct((2, KRYLOV), F32),
-            jax.ShapeDtypeStruct((blocks, MODES, 2 * SPHERES), F32),
+            jax.ShapeDtypeStruct((rows, 2 * SPHERES), F32),
         ),
         in_specs=[anywhere] * 5 + [pl.BlockSpec(memory_space=pltpu.SMEM)],
         out_specs=(pl.BlockSpec(memory_space=pltpu.VMEM),) * 2,
         scratch_shapes=[
-            pltpu.VMEM((KRYLOV, 2, MODES, 128), F32),
-            pltpu.VMEM((2, MODES, 128), F32),
-            pltpu.VMEM((TABLES, MODES, MODES), BF16),
-            pltpu.VMEM((TABLES, 2, MODES, MODES), BF16),
-            pltpu.VMEM((128, 3), jnp.int32),
-            pltpu.VMEM((128, 128), F32),
+            pltpu.VMEM((KRYLOV * rows, 128), F32),
+            pltpu.VMEM((MODES, 2, 128), F32),
+            pltpu.VMEM((2, rows, 128), F32),
+            pltpu.VMEM((MODES, TABLES, MODES), BF16),
+            pltpu.VMEM((TABLES, MODES, 2, MODES), BF16),
+            pltpu.VMEM((TABLES, PAD, PAD), BF16),
+            pltpu.VMEM((TABLES, 2, PAD, PAD), BF16),
+            pltpu.VMEM((3, 1, 128), jnp.int32),
             pltpu.VMEM((2, PAD, 128), F32),
             pltpu.VMEM((3, 8, 128), F32),
             pltpu.VMEM((12, 16, ROWS, PAD), BF16),
-            pltpu.VMEM((8, 32, ROWS, MODES), BF16),
-            pltpu.VMEM((128, MODES), F32),
+            pltpu.VMEM((8, 32, ROWS, PAD), BF16),
             pltpu.VMEM((2, 128, PAD), F32),
-            pltpu.VMEM((2, MODES, 128), F32),
+            pltpu.VMEM((2 * PAD, 128), F32),
+            pltpu.VMEM((rows, 128), F32),
             pltpu.VMEM((2, 8, 8, 128), F32),
             pltpu.VMEM((2, 16, 8, 128), F32),
-            pltpu.SemaphoreType.DMA((6,)),
+            pltpu.SemaphoreType.DMA((13,)),
             pltpu.SemaphoreType.DMA((11 * CHUNKS,)),
             pltpu.SemaphoreType.DMA((12 * CHUNKS,)),
             pltpu.SemaphoreType.DMA((2,)),
@@ -394,7 +416,15 @@
             collective_id=0, has_side_effects=True, vmem_limit_bytes=56 * 1024 * 1024
         ),
         name="arnoldi",
-    )(basis, mie_coeffs, rot_table, axial_table, pair_table, pair_count)
+    )(
+        jnp.transpose(basis, (0, 2, 1, 3)).reshape(KRYLOV * rows, 128),
+        jnp.transpose(mie_coeffs, (1, 0, 2)),
+        jnp.transpose(rot_table, (1, 0, 2)),
+        jnp.transpose(axial_table, (0, 2, 1, 3)),
+        jnp.transpose(pair_table, (2, 0, 1)),
+        pair_count,
+    )
+    return dots, jnp.transpose(vector.reshape(MODES, 2, 128), (1, 0, 2))
 
 
 def solution(mesh):

time: 89.3 us -> 61.8 us (0.69)
  local copies, waits for them, and re-layouts: 23.2 us -> 3.33 us
  Pallas kernels: 64.3 us -> 56.9 us
    unnamed x8 -> x1, local copies, waits for them, and re-layouts: 20.9 us -> 1.2 us
    pallas_call x1, Pallas kernels: 64.3 us -> 56.9 us  [shards(): pl.pallas_call(kernel, out_shape=(jax.ShapeDtypeStruct((2, KRYLOV), F32),...]
    pallas_call x1 -> x0, local copies, waits for them, and re-layouts: 2.23 us -> none  [shards(): pl.pallas_call(kernel, out_shape=(jax.ShapeDtypeStruct((2, KRYLOV), F32),...]
    reshape x0 -> x1, local copies, waits for them, and re-layouts: none -> 2.13 us  [shards(): return (dots, jnp.transpose(vector.reshape(MODES, 2, 128), (1, 0, 2)))]
where the time goes in v2:
time: 61.8 us; the launch traced here: 61.5 us
  Pallas kernels  56.9 us (92%)
  local copies, waits for them, and re-layouts  3.33 us (5%)
  between operations  1.29 us (2%)
    pallas_call x1, Pallas kernels, shards(): pl.pallas_call(kernel, out_shape=(jax.ShapeDtypeStruct((2, KRYLOV), F32),...  56.9 us
    reshape x1, local copies, waits for them, and re-layouts, shards(): return (dots, jnp.transpose(vector.reshape(MODES, 2, 128), (1, 0, 2)))  2.13 us

profile of v2, /device:TPU:1, one launch (start us, length us, event | category | flops | bytes accessed | tf_op | source)
XLA Modules:
  0.0 61.5 jit_solution(13476105884242975961)
XLA Ops:
  1.3 56.9 %arnoldi.1 = (f32[2,8]{1,0:T(2,128)}, f32[1020,128]{1,0:T(8,128)}) custom-call(f32[8160,128]{1,0:T(8,128)} %bitcast.9, f32[510,2,128]{2,1,0:T(2,128)} %bitcast.11, bf16[510,8,510]{2,1,0:T(8,128)(2,1)} %bitcast.10, bf16[8,510,2,510]{3,2,1,0:T(2,128)(2,1)} %bitcast.8, s32[3,1,128]{2,1,0:T(1,128)} %bitcast.13, s32[1]{0:T(128)S(6)} %copy.9.count_ref), custom_call_target="tpu_custom_call" | custom-call | tf_op jit(solution)/shard_map/arnoldi/pallas_call | solution.py:379
  58.2 2.1 %reshape.11 = f32[510,2,128]{2,1,0:T(2,128)} reshape(f32[1020,128]{1,0:T(8,128)} %get-tuple-element.5) | data formatting | bytes 1044480 | tf_op jit(solution)/shard_map/reshape | solution.py:427
  60.3 1.2 %copy.10 = f32[2,8]{1,0:T(2,128)} copy(f32[2,8]{1,0:T(2,128)} %get-tuple-element.8) | data formatting | bytes 128

commit v3 on v2

--- a/solution.py
+++ b/solution.py
@@ -17,7 +17,9 @@
 BLOCKS = 256
 SPHERES = 64
 ROWS = 16
-CHUNKS = 4
+CHUNKS = 2
+LEAST = 0.01
+MOST = 1e37
 MEAN_SCALE = 1.0 / (BLOCKS * MODES * 2 * SPHERES)
 
 NT = (((1,), (1,)), ((), ()))
@@ -82,34 +84,23 @@
     sums[group] = jnp.concatenate(halves, axis=1).astype(BF16)
 
 
-def chain(g, groups, sums, rot, axial):
-    half = len(groups) // 2
-    parts = []
-    for direction in range(2):
+def field_of(sums, operators, field):
+    groups = [[half * 4 + imag * 2 + n for half in range(2) for n in range(2)] for imag in range(2)]
+
+    def gathered(g, direction):
+        parts = []
         for imag in range(2):
             for t in range(2):
-                for n in groups[imag * half : imag * half + half]:
-                    parts.append(sums[n, g * 4 + direction * 2 + t])
-    rotation = rot[g]
-    first, second = axial[g, 0], axial[g, 1]
-    turned = dot(jnp.concatenate(parts, axis=0), rotation, NT).astype(BF16)
-    count = turned.shape[0] // 2
-    forward, backward = turned[:count], turned[count:]
-
-    def swapped(value):
-        return jnp.concatenate([-value[count // 2 :], value[: count // 2]], axis=0)
-
-    moved = dot(forward, first, NT) + dot(swapped(forward), second, NT)
-    moved = moved + dot(backward, first, NN) + dot(swapped(backward), second, NN)
-    return dot(moved.astype(BF16), rotation, NN)
-
-
-def field_of(sums, rot, axial, field):
-    groups = [half * 4 + imag * 2 + n for imag in range(2) for half in range(2) for n in range(2)]
+                parts.extend(sums[n, g * 4 + direction * 2 + t] for n in groups[imag])
+        value = jnp.concatenate(parts, axis=0)
+        return value, jnp.concatenate([-value[128:], value[:128]], axis=0)
+
     total = None
     for g in range(TABLES):
-        value = chain(g, groups, sums, rot, axial)
-        total = value if total is None else total + value
+        for direction, dims in ((0, NT), (1, NN)):
+            for part, value in enumerate(gathered(g, direction)):
+                term = dot(value, operators[g, part], dims)
+                total = term if total is None else total + term
     for imag in range(2):
         for t in range(2):
             start = (imag * 2 + t) * 64
@@ -118,8 +109,8 @@
 
 def kernel(
     basis_hbm, mie_hbm, rot_hbm, axial_hbm, table_hbm, count_ref,
-    proj_ref, out_ref,
-    basis, mie_raw, mie, rot_raw, axial_raw, rot, axial, table, current, pairs, win, sums, field, mixed, image, red_a, red_b,
+    proj_ref, out_ref, norm_ref, flag_ref,
+    basis, mie_raw, mie, rot_raw, axial_raw, rot, axial, operators, table, current, pairs, win, sums, field, mixed, image, red_a, red_b,
     load_sem, send_sem, recv_sem, pair_send, pair_recv, a_send, a_recv, b_send, b_recv,
 ):
     blk_ways, pair_ways = lax.axis_size("blk"), lax.axis_size("pair")
@@ -254,13 +245,39 @@
             value = rot_raw[pl.ds(start, size)]
             rot[:, pl.ds(start, size), pl.ds(0, MODES)] = jnp.swapaxes(value, 0, 1)
 
-    def order_axial(g):
+    def operator(g):
         load_axial[g].wait()
-        axial[g, :, pl.ds(PAD - 16, 16), :] = jnp.zeros((2, 16, PAD), BF16)
-        axial[g, :, :, pl.ds(PAD - 128, 128)] = jnp.zeros((2, PAD, 128), BF16)
+        slot = g % 2
         for start, size in row_pieces(64, MODES):
             value = axial_raw[g, pl.ds(start, size)]
-            axial[g, :, pl.ds(start, size), pl.ds(0, MODES)] = jnp.swapaxes(value, 0, 1)
+            axial[slot, :, pl.ds(start, size), pl.ds(0, MODES)] = jnp.swapaxes(value, 0, 1)
+        rotation = rot[g]
+        flipped = jnp.transpose(rotation)
+        for part in range(2):
+            moved = dot(axial[slot, part], rotation, NN).astype(BF16)
+            operators[g, part] = dot(flipped, moved, NN).astype(BF16)
+
+    def gram():
+        lane = lax.broadcasted_iota(jnp.int32, (1, 128), 1)
+        lines = []
+        for j in range(KRYLOV):
+            real = [jnp.zeros((8, 128), F32)] * KRYLOV
+            imag = [jnp.zeros((8, 128), F32)] * KRYLOV
+            for start, size in row_pieces(64, rows):
+                one = basis[pl.ds(j * rows + start, size), :]
+                turned = times_i(one)
+                for k in range(j, KRYLOV):
+                    other = basis[pl.ds(k * rows + start, size), :]
+                    real[k] = real[k] + fold(one * other)
+                    if k > j:
+                        imag[k] = imag[k] + fold(turned * other)
+            line = jnp.zeros((1, 128), F32)
+            for k in range(j, KRYLOV):
+                line = jnp.where(lane == 8 + k, jnp.sum(real[k]), line)
+                if k > j:
+                    line = jnp.where(lane == 16 + k, jnp.sum(imag[k]), line)
+            lines.append(line)
+        return jnp.concatenate(lines, axis=0)
 
     def order_mie():
         load_mie.wait()
@@ -271,35 +288,35 @@
             mie[0, pl.ds(2 * start, 2 * size), :] = jnp.where(lane < SPHERES, scale, other)
             mie[1, pl.ds(2 * start, 2 * size), :] = jnp.where(lane < SPHERES, other, scale)
 
+    axial[:, :, pl.ds(PAD - 16, 16), :] = jnp.zeros((2, 2, 16, PAD), BF16)
+    axial[:, :, :, pl.ds(PAD - 128, 128)] = jnp.zeros((2, 2, PAD, 128), BF16)
     order_rot()
+    operator(0)
+    operator(1)
     forward(0)
-    order_axial(0)
-    order_axial(1)
+    operator(2)
+    operator(3)
     forward(1)
+    operator(4)
     forward_far(0)
-    order_axial(2)
-    order_axial(3)
-    forward(2)
+    operator(5)
     forward_far(1)
-    order_axial(4)
-    order_axial(5)
-    forward(3)
-    forward_far(2)
-    order_axial(6)
-    order_axial(7)
+    operator(6)
+    operator(7)
     for copy in pair_copies:
         copy.wait()
     counts = count_matrix(pairs, member)
     order_mie()
-    forward_far(3)
+    load_rest.wait()
+    packed_gram = gram()
     landed(range(CHUNKS))
     for group in range(8):
         aggregate(counts, win, sums, group)
-    field_of(sums, rot, axial, field)
-
-    load_rest.wait()
+    field_of(sums, operators, field)
+
     real = [jnp.zeros((8, 128), F32)] * KRYLOV
     imag = [jnp.zeros((8, 128), F32)] * KRYLOV
+    square = jnp.zeros((8, 128), F32)
     for t in range(2):
         mixed[pl.ds(t, PAD, stride=2), :] = jnp.transpose(field[t])
     for start, size in row_pieces(64, rows):
@@ -309,6 +326,7 @@
         value = basis[pl.ds(last * rows + start, size), :] - product
         image[place, :] = value
         turned = times_i(value)
+        square = square + fold(value * value)
         for k in range(KRYLOV):
             vector = basis[pl.ds(k * rows + start, size), :]
             real[k] = real[k] + fold(vector * value)
@@ -334,6 +352,9 @@
                 )
                 copy.start()
                 copies.append(copy)
+            for copy in sends:
+                copy.wait_send()
+            sends.clear()
             for other, device in group:
                 pltpu.make_async_remote_copy(
                     src_ref=store.at[call, other],
@@ -350,11 +371,26 @@
         return value
 
     lane = lax.broadcasted_iota(jnp.int32, (8, 128), 1)
-    packed = jnp.where(lane == 0, tile_of(real), jnp.where(lane == 1, tile_of(imag), 0.0))
-    dots = all_sum(0, packed) * MEAN_SCALE
-    proj_ref[...] = jnp.transpose(dots)[:2]
-
-    square = jnp.zeros((8, 128), F32)
+    packed = jnp.where(lane == 0, tile_of(real), jnp.where(lane == 1, tile_of(imag), packed_gram))
+    packed = jnp.where(lane == 2, jnp.sum(square) * 0.125, packed)
+    reduced = all_sum(0, packed)
+    dots = reduced * MEAN_SCALE
+    turned_dots = jnp.transpose(jnp.concatenate([dots, jnp.zeros((120, 128), F32)], axis=0))
+    proj_ref[...] = turned_dots[:2, :KRYLOV]
+
+    first, second = jnp.where(lane < KRYLOV, turned_dots[0:1], 0.0), jnp.where(lane < KRYLOV, turned_dots[1:2], 0.0)
+    c_real, c_imag = dots[:, 0:1], dots[:, 1:2]
+    weight = jnp.where(lane == lax.broadcasted_iota(jnp.int32, (8, 128), 0), 1.0, 2.0)
+    gram_real, gram_imag = pltpu.roll(reduced, 120, axis=1), pltpu.roll(reduced, 112, axis=1)
+    form = (c_real * first + c_imag * second) * gram_real - (c_real * second - c_imag * first) * gram_imag
+    quadratic = jnp.sum(jnp.where(lane < KRYLOV, weight * form, 0.0)) * MEAN_SCALE
+    linear = 2.0 * jnp.sum(jnp.where(lane < 2, dots * dots, 0.0))
+    constant = jnp.sum(jnp.where(lane == 2, dots, 0.0))
+    norm_square = constant - linear + quadratic
+    fine = (norm_square > LEAST * (constant + linear + quadratic)) & (norm_square < MOST)
+    norm_ref[0] = norm_square
+    flag_ref[0] = jnp.where(fine, 0, 1)
+
     for start, size in row_pieces(64, rows):
         place = pl.ds(start, size)
         plain = image[place, :]
@@ -363,12 +399,7 @@
             vector = basis[pl.ds(k * rows + start, size), :]
             plain = plain - dots[k : k + 1, 0:1] * vector
             turned = turned + dots[k : k + 1, 1:2] * vector
-        value = plain - times_i(turned)
-        image[place, :] = value
-        square = square + fold(value * value)
-    norm_square = jnp.sum(all_sum(1, square)) * MEAN_SCALE
-    scale = lax.rsqrt(jnp.full((8, 128), norm_square, F32))[:1]
-    out_ref[...] = image[...] * scale
+        out_ref[place, :] = plain - times_i(turned)
     for copy in sends:
         copy.wait_send()
 
@@ -376,14 +407,16 @@
 def shards(basis, mie_coeffs, rot_table, axial_table, pair_table, pair_count):
     rows = 2 * MODES
     anywhere = pl.BlockSpec(memory_space=pl.ANY)
-    dots, vector = pl.pallas_call(
+    dots, vector, norm_square, flag = pl.pallas_call(
         kernel,
         out_shape=(
             jax.ShapeDtypeStruct((2, KRYLOV), F32),
             jax.ShapeDtypeStruct((rows, 2 * SPHERES), F32),
+            jax.ShapeDtypeStruct((1,), F32),
+            jax.ShapeDtypeStruct((1,), jnp.int32),
         ),
         in_specs=[anywhere] * 5 + [pl.BlockSpec(memory_space=pltpu.SMEM)],
-        out_specs=(pl.BlockSpec(memory_space=pltpu.VMEM),) * 2,
+        out_specs=(pl.BlockSpec(memory_space=pltpu.VMEM),) * 2 + (pl.BlockSpec(memory_space=pltpu.SMEM),) * 2,
         scratch_shapes=[
             pltpu.VMEM((KRYLOV * rows, 128), F32),
             pltpu.VMEM((MODES, 2, 128), F32),
@@ -391,6 +424,7 @@
             pltpu.VMEM((MODES, TABLES, MODES), BF16),
             pltpu.VMEM((TABLES, MODES, 2, MODES), BF16),
             pltpu.VMEM((TABLES, PAD, PAD), BF16),
+            pltpu.VMEM((2, 2, PAD, PAD), BF16),
             pltpu.VMEM((TABLES, 2, PAD, PAD), BF16),
             pltpu.VMEM((3, 1, 128), jnp.int32),
             pltpu.VMEM((2, PAD, 128), F32),
@@ -400,17 +434,17 @@
             pltpu.VMEM((2, 128, PAD), F32),
             pltpu.VMEM((2 * PAD, 128), F32),
             pltpu.VMEM((rows, 128), F32),
-            pltpu.VMEM((2, 8, 8, 128), F32),
-            pltpu.VMEM((2, 16, 8, 128), F32),
+            pltpu.VMEM((1, 8, 8, 128), F32),
+            pltpu.VMEM((1, 16, 8, 128), F32),
             pltpu.SemaphoreType.DMA((13,)),
             pltpu.SemaphoreType.DMA((11 * CHUNKS,)),
             pltpu.SemaphoreType.DMA((12 * CHUNKS,)),
             pltpu.SemaphoreType.DMA((2,)),
             pltpu.SemaphoreType.DMA((2,)),
-            pltpu.SemaphoreType.DMA((2, 7)),
-            pltpu.SemaphoreType.DMA((2, 8)),
-            pltpu.SemaphoreType.DMA((2, 15)),
-            pltpu.SemaphoreType.DMA((2, 16)),
+            pltpu.SemaphoreType.DMA((1, 7)),
+            pltpu.SemaphoreType.DMA((1, 8)),
+            pltpu.SemaphoreType.DMA((1, 15)),
+            pltpu.SemaphoreType.DMA((1, 16)),
         ],
         compiler_params=pltpu.CompilerParams(
             collective_id=0, has_side_effects=True, vmem_limit_bytes=56 * 1024 * 1024
@@ -424,6 +458,11 @@
         jnp.transpose(pair_table, (2, 0, 1)),
         pair_count,
     )
+    def direct(vector, norm_square):
+        return lax.psum(jnp.sum(vector * vector), ("blk", "pair")) * MEAN_SCALE
+
+    norm_square = lax.cond(flag[0] != 0, direct, lambda vector, norm_square: norm_square, vector, norm_square[0])
+    vector = vector * lax.rsqrt(norm_square)
     return dots, jnp.transpose(vector.reshape(MODES, 2, 128), (1, 0, 2))
 
 

time: 61.8 us -> 50.5 us (0.82)
  Pallas kernels: 56.9 us -> 45.2 us
  between operations: 1.29 us -> 2.54 us
  local copies, waits for them, and re-layouts: 3.33 us -> 2.33 us
    pallas_call x1, Pallas kernels: 56.9 us -> 45.2 us  [shards(): pl.pallas_call(kernel, out_shape=(jax.ShapeDtypeStruct((2, KRYLOV), F32),...]
    reshape x1, local copies, waits for them, and re-layouts: 2.13 us -> 1.09 us  [shards(): return (dots, jnp.transpose(vector.reshape(MODES, 2, 128), (1, 0, 2)))]
where the time goes in v3:
time: 50.5 us; the launch traced here: 50.1 us
  Pallas kernels  45.2 us (90%)
  between operations  2.54 us (5%)
  local copies, waits for them, and re-layouts  2.33 us (5%)
    pallas_call x1, Pallas kernels, shards(): pl.pallas_call(kernel, out_shape=(jax.ShapeDtypeStruct((2, KRYLOV), F32),...  45.2 us
    unnamed x1, local copies, waits for them, and re-layouts  1.24 us
    reshape x1, local copies, waits for them, and re-layouts, shards(): return (dots, jnp.transpose(vector.reshape(MODES, 2, 128), (1, 0, 2)))  1.09 us

profile of v3, /device:TPU:1, one launch (start us, length us, event | category | flops | bytes accessed | tf_op | source)
XLA Modules:
  0.0 50.1 jit_solution(406238738711246181)
XLA Ops:
  1.3 45.2 %arnoldi.1 = (f32[2,8]{1,0:T(2,128)}, f32[1020,128]{1,0:T(8,128)S(1)}, f32[1]{0:T(128)}, s32[1]{0:T(128)}) custom-call(f32[8160,128]{1,0:T(8,128)} %bitcast.11, f32[510,2,128]{2,1,0:T(2,128)} %bitcast.13, bf16[510,8,510]{2,1,0:T(8,128)(2,1)} %bitcast.12, bf16[8,510,2,510]{3,2,1,0:T(2,128)(2,1)} %bitcast.10, s32[3,1,128]{2,1,0:T(1,128)} %bitcast.15, ...), custom_call_target="tpu_custom_call" | custom-call | tf_op jit(solution)/shard_map/arnoldi/pallas_call | solution.py:410
  47.8 1.1 %reshape.15 = f32[510,2,128]{2,1,0:T(2,128)} reshape(f32[1020,128]{1,0:T(8,128)S(1)} %broadcast_multiply_fusion) | data formatting | bytes 1044480 | tf_op jit(solution)/shard_map/reshape | solution.py:466
  48.9 1.2 %copy.13 = f32[2,8]{1,0:T(2,128)} copy(f32[2,8]{1,0:T(2,128)} %get-tuple-element.19) | data formatting | bytes 128
  (2 shorter events, 0.0 us)

commit v4 on v3

--- a/solution.py
+++ b/solution.py
@@ -134,17 +134,19 @@
     ]
     load_rest = pltpu.make_async_copy(basis_hbm.at[head], basis.at[head], load_sem.at[3])
     load_mie = pltpu.make_async_copy(mie_hbm, mie_raw, load_sem.at[4])
-    for load in [load_last, load_table, load_rot, *load_axial, load_rest, load_mie]:
+    for load in [load_last, load_table, load_rot, *load_axial[:4], load_rest, *load_axial[4:], load_mie]:
         load.start()
 
     spot = core * pair_ways + member
     group_a = []
-    for n in range(1, 2 * pair_ways):
+    for n in (2, 6, 1, 3, 5, 7, 4):
         other = lax.rem(spot + n, 2 * pair_ways)
         group_a.append((other, (2 * row + other // pair_ways, lax.rem(other, pair_ways))))
     group_b = []
-    for n in range(1, row_ways):
-        other = lax.rem(row + n, row_ways)
+    high, low = row // 4, lax.rem(row, 4)
+    steps = [(n, m) for n in range(4) for m in range(4) if n or m]
+    for n, m in sorted(steps, key=lambda step: -min(step[0], 4 - step[0]) - min(step[1], 4 - step[1])):
+        other = 4 * lax.rem(high + n, 4) + lax.rem(low + m, 4)
         group_b.append((other, (2 * other + core, member)))
     barrier = pltpu.get_barrier_semaphore()
     for device in [(outer, member)] + [d for _, d in group_a] + [d for _, d in group_b]:
@@ -245,42 +247,40 @@
             value = rot_raw[pl.ds(start, size)]
             rot[:, pl.ds(start, size), pl.ds(0, MODES)] = jnp.swapaxes(value, 0, 1)
 
-    def operator(g):
-        load_axial[g].wait()
-        slot = g % 2
+    def order_axial(g):
         for start, size in row_pieces(64, MODES):
             value = axial_raw[g, pl.ds(start, size)]
-            axial[slot, :, pl.ds(start, size), pl.ds(0, MODES)] = jnp.swapaxes(value, 0, 1)
+            axial[g % 2, :, pl.ds(start, size), pl.ds(0, MODES)] = jnp.swapaxes(value, 0, 1)
+
+    def operator(g):
         rotation = rot[g]
         flipped = jnp.transpose(rotation)
         for part in range(2):
-            moved = dot(axial[slot, part], rotation, NN).astype(BF16)
+            moved = dot(axial[g % 2, part], rotation, NN).astype(BF16)
             operators[g, part] = dot(flipped, moved, NN).astype(BF16)
 
-    def gram():
+    lines = []
+
+    def gram_line(j):
         lane = lax.broadcasted_iota(jnp.int32, (1, 128), 1)
-        lines = []
-        for j in range(KRYLOV):
-            real = [jnp.zeros((8, 128), F32)] * KRYLOV
-            imag = [jnp.zeros((8, 128), F32)] * KRYLOV
-            for start, size in row_pieces(64, rows):
-                one = basis[pl.ds(j * rows + start, size), :]
-                turned = times_i(one)
-                for k in range(j, KRYLOV):
-                    other = basis[pl.ds(k * rows + start, size), :]
-                    real[k] = real[k] + fold(one * other)
-                    if k > j:
-                        imag[k] = imag[k] + fold(turned * other)
-            line = jnp.zeros((1, 128), F32)
+        real = [jnp.zeros((8, 128), F32)] * KRYLOV
+        imag = [jnp.zeros((8, 128), F32)] * KRYLOV
+        for start, size in row_pieces(64, rows):
+            one = basis[pl.ds(j * rows + start, size), :]
+            turned = times_i(one)
             for k in range(j, KRYLOV):
-                line = jnp.where(lane == 8 + k, jnp.sum(real[k]), line)
+                other = basis[pl.ds(k * rows + start, size), :]
+                real[k] = real[k] + fold(one * other)
                 if k > j:
-                    line = jnp.where(lane == 16 + k, jnp.sum(imag[k]), line)
-            lines.append(line)
-        return jnp.concatenate(lines, axis=0)
+                    imag[k] = imag[k] + fold(turned * other)
+        line = jnp.zeros((1, 128), F32)
+        for k in range(j, KRYLOV):
+            line = jnp.where(lane == 8 + k, jnp.sum(real[k]), line)
+            if k > j:
+                line = jnp.where(lane == 16 + k, jnp.sum(imag[k]), line)
+        lines.append(line)
 
     def order_mie():
-        load_mie.wait()
         for start, size in row_pieces(32, MODES):
             scale = mie_raw[pl.ds(start, size)].reshape(2 * size, 128)
             lane = lax.broadcasted_iota(jnp.int32, scale.shape, 1)
@@ -291,24 +291,49 @@
     axial[:, :, pl.ds(PAD - 16, 16), :] = jnp.zeros((2, 2, 16, PAD), BF16)
     axial[:, :, :, pl.ds(PAD - 128, 128)] = jnp.zeros((2, 2, PAD, 128), BF16)
     order_rot()
+    load_axial[0].wait()
+    order_axial(0)
+    load_axial[1].wait()
+    order_axial(1)
     operator(0)
+    load_axial[2].wait()
+    order_axial(2)
     operator(1)
     forward(0)
+    load_axial[3].wait()
+    load_rest.wait()
+    order_axial(3)
     operator(2)
+    gram_line(0)
+    load_axial[4].wait()
+    order_axial(4)
     operator(3)
+    gram_line(1)
     forward(1)
+    load_axial[5].wait()
+    order_axial(5)
     operator(4)
+    gram_line(2)
     forward_far(0)
+    load_axial[6].wait()
+    order_axial(6)
     operator(5)
+    gram_line(3)
     forward_far(1)
-    operator(6)
-    operator(7)
+    load_axial[7].wait()
+    load_mie.wait()
     for copy in pair_copies:
         copy.wait()
+    order_axial(7)
+    operator(6)
+    gram_line(4)
+    gram_line(5)
     counts = count_matrix(pairs, member)
+    operator(7)
+    gram_line(6)
+    gram_line(7)
     order_mie()
-    load_rest.wait()
-    packed_gram = gram()
+    packed_gram = jnp.concatenate(lines, axis=0)
     landed(range(CHUNKS))
     for group in range(8):
         aggregate(counts, win, sums, group)
@@ -376,7 +401,7 @@
     reduced = all_sum(0, packed)
     dots = reduced * MEAN_SCALE
     turned_dots = jnp.transpose(jnp.concatenate([dots, jnp.zeros((120, 128), F32)], axis=0))
-    proj_ref[...] = turned_dots[:2, :KRYLOV]
+    proj_ref[...] = jnp.transpose(jnp.concatenate([reduced, jnp.zeros((120, 128), F32)], axis=0))[:2, :KRYLOV]
 
     first, second = jnp.where(lane < KRYLOV, turned_dots[0:1], 0.0), jnp.where(lane < KRYLOV, turned_dots[1:2], 0.0)
     c_real, c_imag = dots[:, 0:1], dots[:, 1:2]
@@ -463,7 +488,7 @@
 
     norm_square = lax.cond(flag[0] != 0, direct, lambda vector, norm_square: norm_square, vector, norm_square[0])
     vector = vector * lax.rsqrt(norm_square)
-    return dots, jnp.transpose(vector.reshape(MODES, 2, 128), (1, 0, 2))
+    return dots * MEAN_SCALE, jnp.transpose(vector.reshape(MODES, 2, 128), (1, 0, 2))
 
 
 def solution(mesh):

time: 50.5 us -> 49.2 us (0.974)
  other arithmetic: 0.04 us -> 1.28 us
  local copies, waits for them, and re-layouts: 2.33 us -> 1.09 us
  Pallas kernels: 45.2 us -> 44.1 us
    mul x0 -> x1, other arithmetic: none -> 1.24 us  [shards(): dots * MEAN_SCALE]
    unnamed x1 -> x0, local copies, waits for them, and re-layouts: 1.24 us -> none
    pallas_call x1, Pallas kernels: 45.2 us -> 44.1 us  [shards(): pl.pallas_call(kernel, out_shape=(jax.ShapeDtypeStruct((2, KRYLOV), F32),...]
where the time goes in v4:
time: 49.2 us; the launch traced here: 49 us
  Pallas kernels  44.1 us (90%)
  between operations  2.53 us (5%)
  other arithmetic  1.28 us (3%)
  local copies, waits for them, and re-layouts  1.09 us (2%)
    pallas_call x1, Pallas kernels, shards(): pl.pallas_call(kernel, out_shape=(jax.ShapeDtypeStruct((2, KRYLOV), F32),...  44.1 us
    mul x1, other arithmetic, shards(): dots * MEAN_SCALE  1.24 us
    reshape x1, local copies, waits for them, and re-layouts, shards(): vector.reshape(MODES, 2, 128)  1.09 us

profile of v4, /device:TPU:1, one launch (start us, length us, event | category | flops | bytes accessed | tf_op | source)
XLA Modules:
  0.0 49.0 jit_solution(7611598445192655853)
XLA Ops:
  1.3 44.1 %arnoldi.1 = (f32[2,8]{1,0:T(2,128)}, f32[1020,128]{1,0:T(8,128)S(1)}, f32[1]{0:T(128)}, s32[1]{0:T(128)}) custom-call(f32[8160,128]{1,0:T(8,128)} %bitcast.11, f32[510,2,128]{2,1,0:T(2,128)} %bitcast.13, bf16[510,8,510]{2,1,0:T(8,128)(2,1)} %bitcast.12, bf16[8,510,2,510]{3,2,1,0:T(2,128)(2,1)} %bitcast.10, s32[3,1,128]{2,1,0:T(1,128)} %bitcast.15, ...), custom_call_target="tpu_custom_call" | custom-call | tf_op jit(solution)/shard_map/arnoldi/pallas_call | solution.py:435
  46.6 1.2 %broadcast_multiply_fusion.1 = f32[2,8]{1,0:T(2,128)} fusion(f32[2,8]{1,0:T(2,128)} %get-tuple-element.13), kind=kLoop, calls=%fused_computation.2 | loop fusion | flops 16 | bytes 128 | tf_op jit(solution)/shard_map/mul | solution.py:491
  47.9 1.1 %reshape.15 = f32[510,2,128]{2,1,0:T(2,128)} reshape(f32[1020,128]{1,0:T(8,128)S(1)} %broadcast_multiply_fusion) | data formatting | bytes 1044480 | tf_op jit(solution)/shard_map/reshape | solution.py:491
  (2 shorter events, 0.0 us)

commit v5 on v4

--- a/solution.py
+++ b/solution.py
@@ -111,7 +111,7 @@
     basis_hbm, mie_hbm, rot_hbm, axial_hbm, table_hbm, count_ref,
     proj_ref, out_ref, norm_ref, flag_ref,
     basis, mie_raw, mie, rot_raw, axial_raw, rot, axial, operators, table, current, pairs, win, sums, field, mixed, image, red_a, red_b,
-    load_sem, send_sem, recv_sem, pair_send, pair_recv, a_send, a_recv, b_send, b_recv,
+    load_sem, send_sem, recv_sem, pair_send, pair_recv, a_send, a_recv, b_send, b_recv, share_send, share_recv, far_sem,
 ):
     blk_ways, pair_ways = lax.axis_size("blk"), lax.axis_size("pair")
     blk, member = lax.axis_index("blk"), lax.axis_index("pair")
@@ -124,17 +124,19 @@
 
     last = KRYLOV - 1
     rows = 2 * MODES
+    share = TABLES // 2
     first_rows = last * rows // 8 * 8
     head, tail = pl.ds(0, first_rows), pl.ds(first_rows, KRYLOV * rows - first_rows)
     load_last = pltpu.make_async_copy(basis_hbm.at[tail], basis.at[tail], load_sem.at[0])
     load_table = pltpu.make_async_copy(table_hbm, table, load_sem.at[1])
     load_rot = pltpu.make_async_copy(rot_hbm, rot_raw, load_sem.at[2])
     load_axial = [
-        pltpu.make_async_copy(axial_hbm.at[g], axial_raw.at[g], load_sem.at[5 + g]) for g in range(TABLES)
+        pltpu.make_async_copy(axial_hbm.at[core * share + n], axial_raw.at[n], load_sem.at[5 + n])
+        for n in range(share)
     ]
     load_rest = pltpu.make_async_copy(basis_hbm.at[head], basis.at[head], load_sem.at[3])
     load_mie = pltpu.make_async_copy(mie_hbm, mie_raw, load_sem.at[4])
-    for load in [load_last, load_table, load_rot, *load_axial[:4], load_rest, *load_axial[4:], load_mie]:
+    for load in [load_last, load_table, load_rot, *load_axial, load_rest, load_mie]:
         load.start()
 
     spot = core * pair_ways + member
@@ -149,8 +151,15 @@
         other = 4 * lax.rem(high + n, 4) + lax.rem(low + m, 4)
         group_b.append((other, (2 * other + core, member)))
     barrier = pltpu.get_barrier_semaphore()
-    for device in [(outer, member)] + [d for _, d in group_a] + [d for _, d in group_b]:
+    beside_low = [(2 * (4 * high + lax.rem(low + n, 4)) + core, member) for n in (1, 3)]
+    beside_high = [(2 * (4 * lax.rem(high + n, 4) + low) + core, member) for n in (1, 3)]
+    near = [(outer, member)] + [d for _, d in group_a] + beside_low + beside_high
+    for device in near:
         pl.semaphore_signal(barrier, inc=1, device_id=device, device_id_type=MESH)
+
+    def pass_on(turn):
+        for device in beside_high if turn else beside_low:
+            pl.semaphore_signal(far_sem.at[turn], inc=1, device_id=device, device_id_type=MESH)
 
     load_last.wait()
     current[:, pl.ds(MODES - 6, 8), :] = jnp.zeros((2, 8, 128), F32)
@@ -163,17 +172,18 @@
         start = imag * 64 + half * 32 + q * 8
         both = jnp.concatenate([value[start : start + 8] for value in flipped], axis=0)
         win[mine, slab] = both.astype(BF16)
-    pl.semaphore_wait(barrier, 1 + len(group_a) + len(group_b))
+    pl.semaphore_wait(barrier, len(near))
 
     width = 16 // CHUNKS
     sends = []
+    window_sends = list(range(11 * CHUNKS))
 
     def send(source_slot, target_slot, chunk, device):
         place = pl.ds(chunk * width, width)
         copy = pltpu.make_async_remote_copy(
             src_ref=win.at[source_slot, place],
             dst_ref=win.at[target_slot, place],
-            send_sem=send_sem.at[len(sends)],
+            send_sem=send_sem.at[window_sends.pop()],
             recv_sem=recv_sem.at[target_slot * CHUNKS + chunk],
             device_id=device,
             device_id_type=MESH,
@@ -252,12 +262,27 @@
             value = axial_raw[g, pl.ds(start, size)]
             axial[g % 2, :, pl.ds(start, size), pl.ds(0, MODES)] = jnp.swapaxes(value, 0, 1)
 
-    def operator(g):
+    def shared(n, first):
+        place = operators.at[first + n]
+        return pltpu.make_async_remote_copy(
+            src_ref=place,
+            dst_ref=place,
+            send_sem=share_send.at[n],
+            recv_sem=share_recv.at[n],
+            device_id=(inner, member),
+            device_id_type=MESH,
+        )
+
+    def operator(n):
+        g = core * share + n
         rotation = rot[g]
         flipped = jnp.transpose(rotation)
         for part in range(2):
-            moved = dot(axial[g % 2, part], rotation, NN).astype(BF16)
+            moved = dot(axial[n % 2, part], rotation, NN).astype(BF16)
             operators[g, part] = dot(flipped, moved, NN).astype(BF16)
+        copy = shared(n, core * share)
+        copy.start()
+        sends.append(copy)
 
     lines = []
 
@@ -290,50 +315,43 @@
 
     axial[:, :, pl.ds(PAD - 16, 16), :] = jnp.zeros((2, 2, 16, PAD), BF16)
     axial[:, :, :, pl.ds(PAD - 128, 128)] = jnp.zeros((2, 2, PAD, 128), BF16)
+    pass_on(0)
     order_rot()
     load_axial[0].wait()
     order_axial(0)
     load_axial[1].wait()
     order_axial(1)
     operator(0)
+    forward(0)
     load_axial[2].wait()
+    load_rest.wait()
     order_axial(2)
     operator(1)
-    forward(0)
+    gram_line(0)
+    pl.semaphore_wait(far_sem.at[0], 2)
+    pass_on(1)
+    forward(1)
     load_axial[3].wait()
-    load_rest.wait()
     order_axial(3)
     operator(2)
-    gram_line(0)
-    load_axial[4].wait()
-    order_axial(4)
+    gram_line(1)
+    forward_far(0)
+    pl.semaphore_wait(far_sem.at[1], 2)
+    pass_on(2)
     operator(3)
-    gram_line(1)
-    forward(1)
-    load_axial[5].wait()
-    order_axial(5)
-    operator(4)
     gram_line(2)
-    forward_far(0)
-    load_axial[6].wait()
-    order_axial(6)
-    operator(5)
-    gram_line(3)
     forward_far(1)
-    load_axial[7].wait()
     load_mie.wait()
     for copy in pair_copies:
         copy.wait()
-    order_axial(7)
-    operator(6)
-    gram_line(4)
-    gram_line(5)
+    for j in range(3, KRYLOV):
+        gram_line(j)
+    packed_gram = jnp.concatenate(lines, axis=0)
     counts = count_matrix(pairs, member)
-    operator(7)
-    gram_line(6)
-    gram_line(7)
     order_mie()
-    packed_gram = jnp.concatenate(lines, axis=0)
+    pl.semaphore_wait(far_sem.at[2], 2)
+    for n in range(share):
+        shared(n, (1 - core) * share).wait_recv()
     landed(range(CHUNKS))
     for group in range(8):
         aggregate(counts, win, sums, group)
@@ -447,7 +465,7 @@
             pltpu.VMEM((MODES, 2, 128), F32),
             pltpu.VMEM((2, rows, 128), F32),
             pltpu.VMEM((MODES, TABLES, MODES), BF16),
-            pltpu.VMEM((TABLES, MODES, 2, MODES), BF16),
+            pltpu.VMEM((TABLES // 2, MODES, 2, MODES), BF16),
             pltpu.VMEM((TABLES, PAD, PAD), BF16),
             pltpu.VMEM((2, 2, PAD, PAD), BF16),
             pltpu.VMEM((TABLES, 2, PAD, PAD), BF16),
@@ -470,6 +488,9 @@
             pltpu.SemaphoreType.DMA((1, 8)),
             pltpu.SemaphoreType.DMA((1, 15)),
             pltpu.SemaphoreType.DMA((1, 16)),
+            pltpu.SemaphoreType.DMA((TABLES // 2,)),
+            pltpu.SemaphoreType.DMA((TABLES // 2,)),
+            pltpu.SemaphoreType.REGULAR((3,)),
         ],
         compiler_params=pltpu.CompilerParams(
             collective_id=0, has_side_effects=True, vmem_limit_bytes=56 * 1024 * 1024

time: 49.2 us -> 47.1 us (0.957)
  Pallas kernels: 44.1 us -> 42 us
    pallas_call x1, Pallas kernels: 44.1 us -> 42 us  [shards(): pl.pallas_call(kernel, out_shape=(jax.ShapeDtypeStruct((2, KRYLOV), F32),...]
where the time goes in v5:
time: 47.1 us; the launch traced here: 46.9 us
  Pallas kernels  42 us (89%)
  between operations  2.53 us (5%)
  other arithmetic  1.28 us (3%)
  local copies, waits for them, and re-layouts  1.09 us (2%)
    pallas_call x1, Pallas kernels, shards(): pl.pallas_call(kernel, out_shape=(jax.ShapeDtypeStruct((2, KRYLOV), F32),...  42 us
    mul x1, other arithmetic, shards(): dots * MEAN_SCALE  1.24 us
    reshape x1, local copies, waits for them, and re-layouts, shards(): vector.reshape(MODES, 2, 128)  1.09 us

profile of v5, /device:TPU:1, one launch (start us, length us, event | category | flops | bytes accessed | tf_op | source)
XLA Modules:
  0.0 46.9 jit_solution(5097236132881854902)
XLA Ops:
  1.3 42.0 %arnoldi.1 = (f32[2,8]{1,0:T(2,128)}, f32[1020,128]{1,0:T(8,128)S(1)}, f32[1]{0:T(128)}, s32[1]{0:T(128)}) custom-call(f32[8160,128]{1,0:T(8,128)} %bitcast.11, f32[510,2,128]{2,1,0:T(2,128)} %bitcast.13, bf16[510,8,510]{2,1,0:T(8,128)(2,1)} %bitcast.12, bf16[8,510,2,510]{3,2,1,0:T(2,128)(2,1)} %bitcast.10, s32[3,1,128]{2,1,0:T(1,128)} %bitcast.15, ...), custom_call_target="tpu_custom_call" | custom-call | tf_op jit(solution)/shard_map/arnoldi/pallas_call | solution.py:453
  44.5 1.2 %broadcast_multiply_fusion.1 = f32[2,8]{1,0:T(2,128)} fusion(f32[2,8]{1,0:T(2,128)} %get-tuple-element.13), kind=kLoop, calls=%fused_computation.2 | loop fusion | flops 16 | bytes 128 | tf_op jit(solution)/shard_map/mul | solution.py:512
  45.8 1.1 %reshape.15 = f32[510,2,128]{2,1,0:T(2,128)} reshape(f32[1020,128]{1,0:T(8,128)S(1)} %broadcast_multiply_fusion) | data formatting | bytes 1044480 | tf_op jit(solution)/shard_map/reshape | solution.py:512
  (2 shorter events, 0.0 us)

commit v6 on v5

--- a/solution.py
+++ b/solution.py
@@ -151,14 +151,19 @@
         other = 4 * lax.rem(high + n, 4) + lax.rem(low + m, 4)
         group_b.append((other, (2 * other + core, member)))
     barrier = pltpu.get_barrier_semaphore()
-    beside_low = [(2 * (4 * high + lax.rem(low + n, 4)) + core, member) for n in (1, 3)]
-    beside_high = [(2 * (4 * lax.rem(high + n, 4) + low) + core, member) for n in (1, 3)]
-    near = [(outer, member)] + [d for _, d in group_a] + beside_low + beside_high
+    def beside(distance):
+        steps = (distance, row_ways - distance)
+        return [(2 * lax.rem(row + n, row_ways) + core, member) for n in steps]
+
+    near = [(outer, member), (blk, right), (blk, left), (inner, member)]
+    rounds = [near, [(inner, member)] + beside(1), beside(2), beside(4)]
     for device in near:
         pl.semaphore_signal(barrier, inc=1, device_id=device, device_id_type=MESH)
 
     def pass_on(turn):
-        for device in beside_high if turn else beside_low:
+        if turn:
+            pl.semaphore_wait(far_sem.at[turn - 1], len(rounds[turn - 1]))
+        for device in rounds[turn]:
             pl.semaphore_signal(far_sem.at[turn], inc=1, device_id=device, device_id_type=MESH)
 
     load_last.wait()
@@ -167,11 +172,15 @@
     for t in range(2):
         current[t, pl.ds(0, MODES), :] = basis[pl.ds(last * rows + t, MODES, stride=2), :]
     flipped = [jnp.transpose(current[t]) for t in range(2)]
-    for slab in range(16):
-        half, imag, q = slab // 8, slab // 4 % 2, slab % 4
-        start = imag * 64 + half * 32 + q * 8
-        both = jnp.concatenate([value[start : start + 8] for value in flipped], axis=0)
-        win[mine, slab] = both.astype(BF16)
+
+    def place(half):
+        for slab in range(8 * half, 8 * half + 8):
+            start = slab // 4 % 2 * 64 + half * 32 + slab % 4 * 8
+            both = jnp.concatenate([value[start : start + 8] for value in flipped], axis=0)
+            win[mine, slab] = both.astype(BF16)
+
+    place(0)
+    place(1)
     pl.semaphore_wait(barrier, len(near))
 
     width = 16 // CHUNKS
@@ -179,10 +188,10 @@
     window_sends = list(range(11 * CHUNKS))
 
     def send(source_slot, target_slot, chunk, device):
-        place = pl.ds(chunk * width, width)
+        span = pl.ds(chunk * width, width)
         copy = pltpu.make_async_remote_copy(
-            src_ref=win.at[source_slot, place],
-            dst_ref=win.at[target_slot, place],
+            src_ref=win.at[source_slot, span],
+            dst_ref=win.at[target_slot, span],
             send_sem=send_sem.at[window_sends.pop()],
             recv_sem=recv_sem.at[target_slot * CHUNKS + chunk],
             device_id=device,
@@ -192,10 +201,10 @@
         sends.append(copy)
 
     def arrived(slot, chunk):
-        place = pl.ds(chunk * width, width)
+        span = pl.ds(chunk * width, width)
         pltpu.make_async_remote_copy(
-            src_ref=win.at[slot, place],
-            dst_ref=win.at[slot, place],
+            src_ref=win.at[slot, span],
+            dst_ref=win.at[slot, span],
             send_sem=send_sem.at[0],
             recv_sem=recv_sem.at[slot * CHUNKS + chunk],
             device_id=(inner, member),
@@ -232,9 +241,9 @@
     def forward(chunk):
         for origin, keep_on, device in ((left, 0, right), (right, 1, left)):
             arrived(4 + origin, chunk)
-            send(4 + origin, to_outer + origin, chunk, (outer, member))
             if chunk % 2 == keep_on:
                 send(4 + origin, 4 + origin, chunk, (blk, device))
+            send(4 + origin, to_outer + origin, chunk, (outer, member))
             send(4 + origin, to_inner + origin, chunk, (inner, member))
 
     def forward_far(chunk):
@@ -328,19 +337,18 @@
     order_axial(2)
     operator(1)
     gram_line(0)
-    pl.semaphore_wait(far_sem.at[0], 2)
     pass_on(1)
     forward(1)
     load_axial[3].wait()
     order_axial(3)
     operator(2)
+    operator(3)
+    pass_on(2)
+    forward_far(0)
+    forward_far(1)
+    pass_on(3)
     gram_line(1)
-    forward_far(0)
-    pl.semaphore_wait(far_sem.at[1], 2)
-    pass_on(2)
-    operator(3)
     gram_line(2)
-    forward_far(1)
     load_mie.wait()
     for copy in pair_copies:
         copy.wait()
@@ -349,7 +357,7 @@
     packed_gram = jnp.concatenate(lines, axis=0)
     counts = count_matrix(pairs, member)
     order_mie()
-    pl.semaphore_wait(far_sem.at[2], 2)
+    pl.semaphore_wait(far_sem.at[3], len(rounds[3]))
     for n in range(share):
         shared(n, (1 - core) * share).wait_recv()
     landed(range(CHUNKS))
@@ -431,7 +439,7 @@
     constant = jnp.sum(jnp.where(lane == 2, dots, 0.0))
     norm_square = constant - linear + quadratic
     fine = (norm_square > LEAST * (constant + linear + quadratic)) & (norm_square < MOST)
-    norm_ref[0] = norm_square
+    norm_ref[0] = jnp.max(lax.rsqrt(jnp.full((8, 128), norm_square, F32)))
     flag_ref[0] = jnp.where(fine, 0, 1)
 
     for start, size in row_pieces(64, rows):
@@ -450,7 +458,7 @@
 def shards(basis, mie_coeffs, rot_table, axial_table, pair_table, pair_count):
     rows = 2 * MODES
     anywhere = pl.BlockSpec(memory_space=pl.ANY)
-    dots, vector, norm_square, flag = pl.pallas_call(
+    dots, vector, scale, flag = pl.pallas_call(
         kernel,
         out_shape=(
             jax.ShapeDtypeStruct((2, KRYLOV), F32),
@@ -490,7 +498,7 @@
             pltpu.SemaphoreType.DMA((1, 16)),
             pltpu.SemaphoreType.DMA((TABLES // 2,)),
             pltpu.SemaphoreType.DMA((TABLES // 2,)),
-            pltpu.SemaphoreType.REGULAR((3,)),
+            pltpu.SemaphoreType.REGULAR((4,)),
         ],
         compiler_params=pltpu.CompilerParams(
             collective_id=0, has_side_effects=True, vmem_limit_bytes=56 * 1024 * 1024
@@ -504,11 +512,11 @@
         jnp.transpose(pair_table, (2, 0, 1)),
         pair_count,
     )
-    def direct(vector, norm_square):
-        return lax.psum(jnp.sum(vector * vector), ("blk", "pair")) * MEAN_SCALE
-
-    norm_square = lax.cond(flag[0] != 0, direct, lambda vector, norm_square: norm_square, vector, norm_square[0])
-    vector = vector * lax.rsqrt(norm_square)
+    def direct(vector, scale):
+        return lax.rsqrt(lax.psum(jnp.sum(vector * vector), ("blk", "pair")) * MEAN_SCALE)
+
+    scale = lax.cond(flag[0] != 0, direct, lambda vector, scale: scale, vector, scale[0])
+    vector = vector * scale
     return dots * MEAN_SCALE, jnp.transpose(vector.reshape(MODES, 2, 128), (1, 0, 2))
 
 

time: 47.1 us -> 46.6 us (0.989)
  between operations: 2.53 us -> 1.94 us
  other arithmetic: 1.28 us -> 1.84 us
    mul x1, other arithmetic: 0.04 us -> 0.59 us  [shards(): vector = vector * scale]
where the time goes in v6:
time: 46.6 us; the launch traced here: 46.4 us
  Pallas kernels  41.6 us (89%)
  between operations  1.94 us (4%)
  other arithmetic  1.84 us (4%)
  local copies, waits for them, and re-layouts  1.09 us (2%)
    pallas_call x1, Pallas kernels, shards(): pl.pallas_call(kernel, out_shape=(jax.ShapeDtypeStruct((2, KRYLOV), F32),...  41.6 us
    mul x1, other arithmetic, shards(): dots * MEAN_SCALE  1.24 us
    reshape x1, local copies, waits for them, and re-layouts, shards(): vector.reshape(MODES, 2, 128)  1.09 us

profile of v6, /device:TPU:1, one launch (start us, length us, event | category | flops | bytes accessed | tf_op | source)
XLA Modules:
  0.0 46.4 jit_solution(5815159397282048879)
XLA Ops:
  1.3 41.6 %arnoldi.1 = (f32[2,8]{1,0:T(2,128)}, f32[1020,128]{1,0:T(8,128)S(1)}, f32[1]{0:T(128)}, s32[1]{0:T(128)}) custom-call(f32[8160,128]{1,0:T(8,128)} %bitcast.11, f32[510,2,128]{2,1,0:T(2,128)} %bitcast.13, bf16[510,8,510]{2,1,0:T(8,128)(2,1)} %bitcast.12, bf16[8,510,2,510]{3,2,1,0:T(2,128)(2,1)} %bitcast.10, s32[3,1,128]{2,1,0:T(1,128)} %bitcast.15, ...), custom_call_target="tpu_custom_call" | custom-call | tf_op jit(solution)/shard_map/arnoldi/pallas_call | solution.py:461
  43.5 1.2 %broadcast_multiply_fusion.1 = f32[2,8]{1,0:T(2,128)} fusion(f32[2,8]{1,0:T(2,128)} %get-tuple-element.13), kind=kLoop, calls=%fused_computation.2 | loop fusion | flops 16 | bytes 128 | tf_op jit(solution)/shard_map/mul | solution.py:520
  44.8 0.6 %broadcast_multiply_fusion = f32[1020,128]{1,0:T(8,128)S(1)} fusion(f32[1020,128]{1,0:T(8,128)S(1)} %get-tuple-element.14, f32[]{:T(128)} %get-tuple-element.17), kind=kLoop, calls=%fused_computation.1 | loop fusion | flops 130560 | bytes 1044484 | tf_op jit(solution)/shard_map/mul | solution.py:519
  45.4 1.1 %reshape.15 = f32[510,2,128]{2,1,0:T(2,128)} reshape(f32[1020,128]{1,0:T(8,128)S(1)} %broadcast_multiply_fusion) | data formatting | bytes 1044480 | tf_op jit(solution)/shard_map/reshape | solution.py:520
  (1 shorter events, 0.0 us)

commit v7 on v6

--- a/solution.py
+++ b/solution.py
@@ -331,17 +331,17 @@
     load_axial[1].wait()
     order_axial(1)
     operator(0)
-    forward(0)
     load_axial[2].wait()
-    load_rest.wait()
     order_axial(2)
     operator(1)
+    forward(0)
+    load_axial[3].wait()
+    load_rest.wait()
+    order_axial(3)
+    operator(2)
     gram_line(0)
     pass_on(1)
     forward(1)
-    load_axial[3].wait()
-    order_axial(3)
-    operator(2)
     operator(3)
     pass_on(2)
     forward_far(0)

time: 46.6 us -> 47.1 us (1.011)
  Pallas kernels: 41.6 us -> 42.1 us
    pallas_call x1, Pallas kernels: 41.6 us -> 42.1 us  [shards(): pl.pallas_call(kernel, out_shape=(jax.ShapeDtypeStruct((2, KRYLOV), F32),...]
where the time goes in v7:
time: 47.1 us; the launch traced here: 47 us
  Pallas kernels  42.1 us (89%)
  between operations  1.94 us (4%)
  other arithmetic  1.84 us (4%)
  local copies, waits for them, and re-layouts  1.09 us (2%)
    pallas_call x1, Pallas kernels, shards(): pl.pallas_call(kernel, out_shape=(jax.ShapeDtypeStruct((2, KRYLOV), F32),...  42.1 us
    mul x1, other arithmetic, shards(): dots * MEAN_SCALE  1.24 us
    reshape x1, local copies, waits for them, and re-layouts, shards(): vector.reshape(MODES, 2, 128)  1.09 us

profile of v7, /device:TPU:1, one launch (start us, length us, event | category | flops | bytes accessed | tf_op | source)
XLA Modules:
  0.0 47.0 jit_solution(4339971896388656961)
XLA Ops:
  1.3 42.1 %arnoldi.1 = (f32[2,8]{1,0:T(2,128)}, f32[1020,128]{1,0:T(8,128)S(1)}, f32[1]{0:T(128)}, s32[1]{0:T(128)}) custom-call(f32[8160,128]{1,0:T(8,128)} %bitcast.11, f32[510,2,128]{2,1,0:T(2,128)} %bitcast.13, bf16[510,8,510]{2,1,0:T(8,128)(2,1)} %bitcast.12, bf16[8,510,2,510]{3,2,1,0:T(2,128)(2,1)} %bitcast.10, s32[3,1,128]{2,1,0:T(1,128)} %bitcast.15, ...), custom_call_target="tpu_custom_call" | custom-call | tf_op jit(solution)/shard_map/arnoldi/pallas_call | solution.py:461
  44.0 1.2 %broadcast_multiply_fusion.1 = f32[2,8]{1,0:T(2,128)} fusion(f32[2,8]{1,0:T(2,128)} %get-tuple-element.13), kind=kLoop, calls=%fused_computation.2 | loop fusion | flops 16 | bytes 128 | tf_op jit(solution)/shard_map/mul | solution.py:520
  45.3 0.6 %broadcast_multiply_fusion = f32[1020,128]{1,0:T(8,128)S(1)} fusion(f32[1020,128]{1,0:T(8,128)S(1)} %get-tuple-element.14, f32[]{:T(128)} %get-tuple-element.17), kind=kLoop, calls=%fused_computation.1 | loop fusion | flops 130560 | bytes 1044484 | tf_op jit(solution)/shard_map/mul | solution.py:519
  45.9 1.1 %reshape.15 = f32[510,2,128]{2,1,0:T(2,128)} reshape(f32[1020,128]{1,0:T(8,128)S(1)} %broadcast_multiply_fusion) | data formatting | bytes 1044480 | tf_op jit(solution)/shard_map/reshape | solution.py:520
  (1 shorter events, 0.0 us)
